TPU v7x, 128 devices: a whole 4x4x4 slice. The times are simulated.
128 devices in a mesh: section: 2 (over y_hi), seq: 16 (over z, y_lo, core), mp: 4 (over x).
Axes of the slice: x: 4, y: 4 (y_hi: 2, y_lo: 2; y = y_hi * 2 + y_lo), z: 4, core: 2. Of those that a mesh axis runs over, the one named last changes fastest.
Arguments:
- patches: bfloat16 [16384, 1280], P('seq'), may hold values from -6 to 6
- norm_gain: bfloat16 [1280], replicated, may hold values from 0.099609375 to 1.8984375
- norm_shift: bfloat16 [1280], replicated, may hold values from -3 to 3
- merge_in_weight: bfloat16 [5120, 5120], P(None, ('section', 'mp')), may hold values from -0.078125 to 0.078125
- merge_in_bias: bfloat16 [5120], P(('section', 'mp')), may hold values from -3 to 3
- merge_out_weight: bfloat16 [5120, 8192], P(('section', 'mp'), 'seq'), may hold values from -0.078125 to 0.078125
- merge_out_bias: bfloat16 [8192], P('seq'), may hold values from -3 to 3
- text_embeds: bfloat16 [6144, 8192], P('seq', 'mp'), may hold values from -6 to 6
- rms_gain: bfloat16 [8192], replicated, may hold values from 0.099609375 to 1.8984375
- query_weight: bfloat16 [8192, 4096], P(None, ('section', 'mp')), may hold values from -0.0625 to 0.0625
- query_bias: bfloat16 [4096], P(('section', 'mp')), may hold values from -12 to 12
- key_weight: bfloat16 [8192, 512], P(None, 'mp'), may hold values from -0.0625 to 0.0625
- key_bias: bfloat16 [512], P('mp'), may hold values from -12 to 12
- value_weight: bfloat16 [8192, 512], P(None, 'mp'), may hold values from -0.0625 to 0.0625
- value_bias: bfloat16 [512], P('mp'), may hold values from -3 to 3
- patch_counts: int32 [16], replicated, may hold values from 256 to 1024, as said below
- image_offsets: int32 [16], replicated, may hold values from 0 to 6080, as said below
Outputs:
- sequence_embeds: bfloat16 [6144, 8192], P('seq', 'mp')
- context: bfloat16 [6144, 4096], P('seq', ('section', 'mp'))
Inputs may be any that keep to these rules, and one draw needn't show every extreme that they name: `patch_counts`: multiples of 4; in every draw one image has exactly 1024 patches and another exactly a quarter of 1024. Image i's merged tokens occupy positions image_offsets[i] to image_offsets[i] + patch_counts[i] / 4 - 1; these ranges rise with i, do not intersect and lie inside the sequence; the first image starts at position 0 and the last image ends at the sequence's last position.
All inputs are finite; a program needn't handle non-finite values.
Results may differ from a plain program's by a relative error of at most 0.012.
The roundings to bfloat16 on the way count: a program that leaves them out, or rounds other values in their place, can miss the bound.
Values may be sent and summed in bfloat16 or wider, within the bound.
A program may use at most 384 MiB of HBM per device.

v0:
```python
import math

import jax
import jax.numpy as jnp
from jax import lax
from jax.sharding import PartitionSpec as P

HEAD = 128


def layer_norm(inputs, scale_vec, shift_vec):
    values = inputs.astype(jnp.float32)
    center = values - jnp.mean(values, axis=-1, keepdims=True)
    spread = jnp.mean(center * center, axis=-1, keepdims=True)
    normed = center * lax.rsqrt(spread + 1e-06) * scale_vec.astype(jnp.float32) + shift_vec.astype(
        jnp.float32
    )
    return normed.astype(jnp.bfloat16)


def rms_norm(inputs, scale_vec):
    values = inputs.astype(jnp.float32)
    square_mean = jnp.mean(values * values, axis=-1, keepdims=True)
    return (values * lax.rsqrt(square_mean + 1e-06) * scale_vec.astype(jnp.float32)).astype(
        jnp.bfloat16
    )


def rotate(values, positions):
    half_dim = values.shape[-1] // 2
    inv_freq = jnp.exp(
        jnp.arange(half_dim, dtype=jnp.float32) * (-2.0 * math.log(1000000.0) / values.shape[-1])
    )
    angles = positions.astype(jnp.float32)[:, None] * inv_freq[None, :]
    cosine = jnp.cos(angles)[:, None, :]
    sine_vals = jnp.sin(angles)[:, None, :]
    lower_half = values[..., :half_dim]
    upper_half = values[..., half_dim:]
    return jnp.concatenate(
        [
            lower_half * cosine - upper_half * sine_vals,
            upper_half * cosine + lower_half * sine_vals,
        ],
        axis=-1,
    )


def project(normed_seq, weight, bias_vec, positions, rotary):
    values = jnp.dot(normed_seq, weight, preferred_element_type=jnp.float32) + bias_vec.astype(
        jnp.float32
    )
    values = values.reshape(values.shape[0], -1, HEAD)
    if rotary:
        values = rotate(values, positions)
    return values.astype(jnp.bfloat16)


def visual_slots(positions, counts, offsets, per_image):
    relative = positions[:, None] - offsets[None, :]
    inside = (relative >= 0) & (relative < (counts // 4)[None, :])
    images = jnp.arange(counts.shape[0], dtype=jnp.int32)
    slot_rows = jnp.sum(jnp.where(inside, images[None, :] * per_image + relative, 0), axis=1)
    return (slot_rows, jnp.any(inside, axis=1))


def local(
    patches,
    norm_gain,
    norm_shift,
    merge_in_weight,
    merge_in_bias,
    merge_out_weight,
    merge_out_bias,
    text_embeds,
    rms_gain,
    query_weight,
    query_bias,
    key_weight,
    key_bias,
    value_weight,
    value_bias,
    patch_counts,
    image_offsets,
):
    per_image = patches.shape[0] // 4
    normed = layer_norm(patches, norm_gain, norm_shift)
    merged = normed.reshape(per_image, 4 * patches.shape[1])
    hidden = jax.nn.gelu(
        jnp.dot(merged, merge_in_weight, preferred_element_type=jnp.float32)
        + merge_in_bias.astype(jnp.float32),
        approximate=False,
    ).astype(jnp.bfloat16)
    gathered = lax.all_gather(hidden, "seq", axis=0, tiled=True)
    seq_count = lax.axis_size("seq")
    own_rows = text_embeds.shape[0]
    length = own_rows * seq_count
    positions = jnp.arange(length, dtype=jnp.int32)
    slot_rows, is_visual = visual_slots(positions, patch_counts, image_offsets, per_image)
    partial_value = jnp.dot(
        jnp.take(gathered, slot_rows, axis=0), merge_out_weight, preferred_element_type=jnp.float32
    )
    leading = (lax.axis_index(("section", "mp")) == 0).astype(jnp.float32)
    partial_value = partial_value + leading * merge_out_bias.astype(jnp.float32)[None, :]
    col_width = text_embeds.shape[1]
    routed = lax.all_to_all(partial_value, "seq", split_axis=0, concat_axis=1, tiled=True)
    visual = lax.psum(routed, ("section", "mp")).astype(jnp.bfloat16)
    visual_cols = lax.dynamic_slice_in_dim(visual, lax.axis_index("mp") * col_width, col_width, 1)
    first_row = lax.axis_index("seq") * own_rows
    own_positions = first_row + jnp.arange(own_rows, dtype=jnp.int32)
    own_visual = lax.dynamic_slice_in_dim(is_visual, first_row, own_rows, 0)
    embeds = jnp.where(own_visual[:, None], visual_cols, text_embeds)
    whole_rows = lax.all_gather(embeds, "mp", axis=1, tiled=True)
    normed_seq = rms_norm(whole_rows, rms_gain)
    queries = project(normed_seq, query_weight, query_bias, own_positions, True)
    own_keys = project(normed_seq, key_weight, key_bias, own_positions, True)[:, 0, :]
    own_values = project(normed_seq, value_weight, value_bias, own_positions, False)[:, 0, :]
    all_keys, all_values = (
        lax.all_gather(own_keys, "seq", axis=0, tiled=True),
        lax.all_gather(own_values, "seq", axis=0, tiled=True),
    )
    score_scale = HEAD ** (-0.5)
    scores = (
        jnp.einsum("shd,kd->hsk", queries, all_keys, preferred_element_type=jnp.float32)
        * score_scale
    )
    causal = positions[None, None, :] <= own_positions[None, :, None]
    scores = jnp.where(causal, scores, -jnp.inf)
    row_max = jnp.max(scores, axis=2, keepdims=True)
    exp_scores = jnp.exp(scores - row_max)
    weights = (exp_scores / jnp.sum(exp_scores, axis=2, keepdims=True)).astype(jnp.bfloat16)
    context = jnp.einsum(
        "hsk,kd->shd", weights, all_values, preferred_element_type=jnp.float32
    ).astype(jnp.bfloat16)
    return (embeds, context.reshape(own_rows, -1))


def solution(mesh):
    placed = (
        P("seq", None),
        P(),
        P(),
        P(None, ("section", "mp")),
        P(("section", "mp")),
        P(("section", "mp"), "seq"),
        P("seq"),
        P("seq", "mp"),
        P(),
        P(None, ("section", "mp")),
        P(("section", "mp")),
        P(None, "mp"),
        P("mp"),
        P(None, "mp"),
        P("mp"),
        P(),
        P(),
    )
    return jax.shard_map(
        local,
        mesh=mesh,
        in_specs=placed,
        out_specs=(P("seq", "mp"), P("seq", ("section", "mp"))),
        check_vma=False,
    )
```

profile of v0, /device:TPU:105, one launch (start us, length us, event | category | flops | bytes accessed | tf_op | source)
XLA Modules:
  0.0 785.5 jit_solution(13626968816766021919)
XLA Ops:
  7.2 0.0 all-gather.5.cloned.1.call-start
  7.2 0.8 convert_element_type.75
  8.1 2.2 convert_reduce_fusion
  10.3 2.6 fusion.10
  12.9 0.7 convert_element_type.72
  13.6 0.7 convert_element_type.73
  14.3 2.5 fusion.13
  16.8 5.2 reshape.222
  22.1 8.0 %fusion.26 = bf16[256,640]{1,0:T(8,128)(2,1)} fusion(bf16[256,5120]{1,0:T(8,128)(2,1)} %reshape.222, bf16[5120,640]{1,0:T(8,128)(2,1)} %param.20, f32[640]{0:T(1024)S(1)} %convert_element_type.75), kind=kOutput, calls=%fused_computation.42 | convolution fusion | flops 1688535040 | bytes 9505280 | tf_op jit(solution)/shard_map/dot_general | solution.py:89
  30.0 0.0 all-gather.5.cloned.1.call-update
  30.1 0.2 select_reduce_fusion
  30.4 39.0 %all-gather.5.cloned.1.call-done = bf16[4096,640]{1,0:T(8,128)(2,1)} async-done(((bf16[256,640]{1,0:T(8,128)(2,1)}), bf16[4096,640]{1,0:T(8,128)(2,1)}) %all-gather.5.cloned.1.call-update) | async-done | bytes 5242896 | tf_op jit(solution)/shard_map/all_gather | solution.py:93
  69.4 29.7 %gather_fusion = bf16[6144,640]{1,0:T(8,128)(2,1)} fusion(bf16[4096,640]{1,0:T(8,128)(2,1)} %all-gather.5.cloned.1.call-done, s32[6144]{0:T(1024)S(1)} %broadcast_clamp_fusion), kind=kCustom, calls=%fused_computation | custom fusion | bytes 15753216 | tf_op jit(solution)/shard_map/jit(_take)/gather | solution.py:100
  99.1 10.1 %convolution_add_fusion = f32[6144,512]{1,0:T(8,128)} fusion(bf16[640,512]{1,0:T(8,128)(2,1)S(1)} %copy-done.8, bf16[6144,640]{1,0:T(8,128)(2,1)} %gather_fusion, pred[6144]{0:T(1024)(128)(4,1)S(1)} %compare_and_fusion, f32[512]{0:T(512)S(1)} %convert_multiply_fusion.2), kind=kOutput, calls=%fused_computation.13 | convolution fusion | flops 4033609728 | bytes 21110784 | tf_op jit(solution)/shard_map/dot_general | solution.py:99
  109.2 6.8 all-to-all-start
  116.0 0.2 all-gather.7.cloned.1.call-start
  116.3 0.2 fusion.40
  116.4 0.1 dynamic_slice.6
  116.5 136.0 %all-to-all-done = f32[16,384,512]{2,1,0:T(8,128)} async-done(((f32[16,384,512]{2,1,0:T(8,128)}), f32[16,384,512]{2,1,0:T(8,128)}, u32[]{:S(2)}, u32[]{:S(2)}) %all-to-all-start) | async-done | bytes 12582944 | tf_op jit(solution)/shard_map/all_to_all | solution.py:105
  252.6 11.3 %copy.45 = f32[16,48,8,512]{3,2,0,1:T(8,128)} copy(f32[16,48,8,512]{3,2,1,0:T(8,128)} %bitcast.13) | data formatting | bytes 25165824 | tf_op jit(solution)/shard_map/all_to_all | solution.py:105
  263.9 252.3 %all-reduce.1 = bf16[384,8192]{1,0:T(8,128)(2,1)} all-reduce(f32[384,8192]{1,0:T(8,128)} %bitcast.40), channel_id=1, replica_groups=mesh['section'=2,'seq'=16,'mp'=4] {'section','mp'}, use_global_device_ids=true, to_apply=%region_4.5 | all-reduce | flops 3145728 | bytes 18874368 | tf_op jit(solution)/shard_map/psum | solution.py:106
  516.2 3.5 fusion.15
  519.6 0.0 all-gather.7.cloned.1.call-update
  519.6 0.0 all-gather.11.cloned.1.call-start
  519.8 66.8 %all-gather.7.cloned.1.call-done = bf16[384,8192]{1,0:T(8,128)(2,1)} async-done(((bf16[384,2048]{1,0:T(8,128)(2,1)}), bf16[384,8192]{1,0:T(8,128)(2,1)}) %all-gather.7.cloned.1.call-update) | async-done | bytes 6291472 | tf_op jit(solution)/shard_map/all_gather | solution.py:112
  586.6 4.1 fusion.3
  590.7 5.1 fusion.22
  595.9 0.4 fusion.50
  596.3 0.7 pad_maximum_fusion
  597.0 0.0 all-gather.11.cloned.1.call-update
  597.0 0.0 all-gather.9.cloned.1.call-start
  597.0 3.2 iota_compare_fusion
  600.3 0.8 multiply_cosine_fusion
  601.0 8.1 %convolution_add_fusion.1 = f32[384,512]{1,0:T(8,128)S(1)} fusion(bf16[8192,512]{1,0:T(8,128)(2,1)} %param.26, f32[512]{0:T(512)S(1)} %convert_element_type.87, bf16[384,8192]{1,0:T(8,128)(2,1)} %all-gather.7.cloned.1.call-done, f32[8192]{0:T(1024)S(1)} %convert_element_type.81, f32[384]{0:T(512)S(1)} %add_rsqrt_fusion.1), kind=kOutput, calls=%fused_computation.30 | convolution fusion | flops 3234004992 | bytes 15502848 | tf_op jit(solution)/shard_map/dot_general | solution.py:49
  609.1 0.3 reshape.224
  609.4 0.5 fusion.57
  609.9 6.0 fusion.23
  615.9 0.0 all-gather.9.cloned.1.call-update
  615.9 0.2 subtract_convert_fusion
  616.1 13.8 %all-gather.11.cloned.1.call-done = bf16[6144,128]{0,1:T(8,128)(2,1)} async-done(((bf16[384,128]{0,1:T(8,128)(2,1)}), bf16[6144,128]{0,1:T(8,128)(2,1)}) %all-gather.11.cloned.1.call-update) | async-done | bytes 1572880 | tf_op jit(solution)/shard_map/all_gather | solution.py:118
  629.9 16.5 %fusion.16 = f32[6144,384,4]{1,0,2:T(8,128)} fusion(bf16[6144,128]{0,1:T(8,128)(2,1)} %all-gather.11.cloned.1.call-done, bf16[384,4,64]{2,0,1:T(8,128)(2,1)S(1)} %get-tuple-element.9, bf16[384,4,64]{2,0,1:T(8,128)(2,1)S(1)} %get-tuple-element.8), kind=kOutput, calls=%fused_computation.27 | convolution fusion | flops 2416705536 | bytes 39714816 | tf_op jit(solution)/shard_map/shd,kd->hsk/dot_general | solution.py:123
  646.4 4.7 broadcast_in_dim.31
  651.1 12.5 %mul.213 = f32[6144,384,4]{1,0,2:T(8,128)} broadcast(f32[]{:T(128)} %constant.136.clone.1), dimensions={} | broadcast | bytes 37748740 | tf_op jit(solution)/shard_map/mul | solution.py:123
  663.6 12.4 %broadcast_in_dim.32 = f32[4,384,6144]{1,2,0:T(8,128)} broadcast(f32[]{:T(128)} %constant.137.clone.1), dimensions={} | broadcast | bytes 37748740 | tf_op jit(solution)/shard_map/jit(_where)/broadcast_in_dim | solution.py:127
  676.0 88.2 %fusion.58 = (f32[4,384]{1,0:T(4,128)S(1)}, f32[4,384,6144]{1,2,0:T(8,128)}) fusion(pred[4,384,6144]{1,2,0:T(8,128)(4,1)} %broadcast_in_dim.31, f32[4,384,6144]{1,2,0:T(8,128)} %broadcast_in_dim.32, f32[6144,384,4]{1,0,2:T(8,128)} %fusion.16, f32[6144,384,4]{1,0,2:T(8,128)} %mul.213), kind=kOutput, calls=%fused_computation.101 | output fusion | flops 56629248 | bytes 160438272 | tf_op jit(solution)/shard_map/sub | solution.py:129
  764.2 0.0 all-gather.9.cloned.1.call-done
  764.3 13.8 %fusion.19 = bf16[128,4,384]{2,0,1:T(8,128)(2,1)S(1)} fusion(f32[4,384,6144]{1,2,0:T(8,128)} %get-tuple-element.17, f32[4,384]{1,0:T(4,128)S(1)} %get-tuple-element.16, bf16[6144,128]{1,0:T(8,128)(2,1)} %all-gather.9.cloned.1.call-done), kind=kOutput, calls=%fused_computation.31 | convolution fusion | flops 2434990080 | bytes 39720960 | tf_op jit(solution)/shard_map/hsk,kd->shd/dot_general | solution.py:131
  778.0 0.9 copy.37
  (39 shorter events, 0.2 us)
Async XLA Ops:
  7.2 583.5 %copy-start = (bf16[8192,128]{1,0:T(8,128)(2,1)S(1)}, bf16[8192,128]{1,0:T(8,128)(2,1)}, u32[]{:S(2)}) copy-start(bf16[8192,128]{1,0:T(8,128)(2,1)} %param.28) | copy-start | bytes 6291460
  7.2 62.2 %all-gather.5.cloned.1.call-start = ((), (), s32[]{:S(2)}) async-start(), calls=%async_computation.1 | async-start | bytes 5570560 | tf_op jit(solution)/shard_map/all_gather | solution.py:93
  7.2 7.1 copy-start.2
  22.0 8.0 %copy-start.9 = (s32[16]{0:T(128)S(1)}, s32[16]{0:T(128)}, u32[]{:S(2)}) copy-start(s32[16]{0:T(128)} %param.32) | copy-start | bytes 196
  22.0 8.0 %copy-start.5 = (s32[16]{0:T(128)S(1)}, s32[16]{0:T(128)}, u32[]{:S(2)}) copy-start(s32[16]{0:T(128)} %param.33) | copy-start | bytes 196
  22.1 8.2 %copy-start.6 = (bf16[512]{0:T(512)(128)(2,1)S(1)}, bf16[512]{0:T(512)(128)(2,1)}, u32[]{:S(2)}) copy-start(bf16[512]{0:T(512)(128)(2,1)} %param.23) | copy-start | bytes 3076
  30.4 68.7 %copy-start.8 = (bf16[640,512]{1,0:T(8,128)(2,1)S(1)}, bf16[640,512]{1,0:T(8,128)(2,1)}, u32[]{:S(2)}) copy-start(bf16[640,512]{1,0:T(8,128)(2,1)} %param.22) | copy-start | bytes 1966084
  109.2 143.3 %all-to-all-start = ((f32[16,384,512]{2,1,0:T(8,128)}), f32[16,384,512]{2,1,0:T(8,128)}, u32[]{:S(2)}, u32[]{:S(2)}) async-start(f32[16,384,512]{2,1,0:T(8,128)} %bitcast.41), calls=%async_computation | async-start | bytes 25165824 | tf_op jit(solution)/shard_map/all_to_all | solution.py:105
  116.0 470.6 %all-gather.7.cloned.1.call-start = ((), (), s32[]{:S(2)}) async-start(), calls=%async_computation.2 | async-start | bytes 7864320 | tf_op jit(solution)/shard_map/all_gather | solution.py:112
  263.9 255.8 %copy-start.10 = (bf16[128]{0:T(256)(128)(2,1)S(1)}, bf16[128]{0:T(256)(128)(2,1)}, u32[]{:S(2)}) copy-start(bf16[128]{0:T(256)(128)(2,1)} %param.29) | copy-start | bytes 772
  263.9 255.9 %copy-start.4 = (bf16[8192]{0:T(1024)(128)(2,1)S(1)}, bf16[8192]{0:T(1024)(128)(2,1)}, u32[]{:S(2)}) copy-start(bf16[8192]{0:T(1024)(128)(2,1)} %param.25) | copy-start | bytes 49156
  519.6 110.2 %all-gather.11.cloned.1.call-start = ((), (), s32[]{:S(2)}) async-start(), calls=%async_computation.4 | async-start | bytes 1671168 | tf_op jit(solution)/shard_map/all_gather | solution.py:118
  590.7 9.5 %copy-start.11 = (bf16[128]{0:T(256)(128)(2,1)S(1)}, bf16[128]{0:T(256)(128)(2,1)}, u32[]{:S(2)}) copy-start(bf16[128]{0:T(256)(128)(2,1)} %param.31) | copy-start | bytes 772
  590.7 9.5 %copy-start.7 = (bf16[512]{0:T(512)(128)(2,1)S(1)}, bf16[512]{0:T(512)(128)(2,1)}, u32[]{:S(2)}) copy-start(bf16[512]{0:T(512)(128)(2,1)} %param.27) | copy-start | bytes 3076
  597.0 167.3 %all-gather.9.cloned.1.call-start = ((), (), s32[]{:S(2)}) async-start(), calls=%async_computation.3 | async-start | bytes 1671168 | tf_op jit(solution)/shard_map/all_gather | solution.py:119
  629.9 16.5 %copy-start.3 = (pred[384,6144]{0,1:T(8,128)(4,1)S(1)}, pred[384,6144]{0,1:T(8,128)(4,1)}, u32[]{:S(2)}) copy-start(pred[384,6144]{0,1:T(8,128)(4,1)} %iota_compare_fusion) | copy-start | bytes 7077892
  764.2 14.7 %copy-start.1 = (bf16[8192,128]{1,0:T(8,128)(2,1)S(1)}, bf16[8192,128]{1,0:T(8,128)(2,1)}, u32[]{:S(2)}) copy-start(bf16[8192,128]{1,0:T(8,128)(2,1)} %param.28) | copy-start | bytes 6291460
Sparse Core Ops, SparseCore 0:
  30.1 39.2 all-gather.4
  519.8 66.7 all-gather.6
  597.1 32.7 all-gather.10
  631.5 33.2 all-gather.8
where the time goes:
time: 790 us; the launch traced here: 786 us
  waiting for transfers between devices  256 us (32%)
  blocking collectives  252 us (32%)
  other arithmetic  111 us (14%)
  local copies, waits for them, and re-layouts  77.6 us (10%)
  matrix products  67.6 us (9%)
  between operations  14 us (2%)
    psum x1, blocking collectives, local(): visual = lax.psum(routed, ('section', 'mp')).astype(jnp.bfloat16)  252 us
    all_to_all x1, waiting for transfers between devices, local(): lax.all_to_all(partial_value, 'seq', split_axis=0, concat_axis=1, tiled=T...  136 us
    sub x1, other arithmetic, local(): exp_scores = jnp.exp(scores - row_max)  88.2 us
    all_gather x1, waiting for transfers between devices, local(): whole_rows = lax.all_gather(embeds, 'mp', axis=1, tiled=True)  66.8 us
    all_gather x1, waiting for transfers between devices, local(): gathered = lax.all_gather(hidden, 'seq', axis=0, tiled=True)  39 us
    gather x1, local copies, waits for them, and re-layouts, local(): jnp.take(gathered, slot_rows, axis=0)  29.7 us
    dot_general x3, matrix products, project(): jnp.dot(normed_seq, weight, preferred_element_type=jnp.float32)  19.2 us
    broadcast_in_dim x2, local copies, waits for them, and re-layouts, local(): scores = jnp.where(causal, scores, -jnp.inf)  17.1 us
  transfers between devices with their start and end apart: 5, of which 4 were waited for; matrix products, arithmetic and copies ran while one was open for 20% of the time, Pallas kernels for 0%

commit v1 on v0

v1 whole, which is shorter than its diff:
```python
import functools
import math

import jax
import jax.numpy as jnp
from jax import lax
from jax.experimental import pallas as pl
from jax.experimental.pallas import tpu as pltpu
from jax.sharding import PartitionSpec as P

HEAD = 128
MESH = pl.DeviceIdType.MESH
MIB = 1024 * 1024
ANY = pl.BlockSpec(memory_space=pl.ANY)
VMEM = pl.BlockSpec(memory_space=pltpu.VMEM)
BF16 = jnp.bfloat16
F32 = jnp.float32


def coords():
    s = lax.axis_index("section")
    q = lax.axis_index("seq")
    z = lax.div(q, 4)
    y = s * 2 + lax.rem(lax.div(q, 2), 2)
    return z, y, lax.rem(q, 2), lax.axis_index("mp")


def place(z, y, c):
    return lax.div(y, 2), z * 4 + lax.rem(y, 2) * 2 + c


def device(z, y, c, x):
    s, q = place(z, y, c)
    return {"section": s, "seq": q, "mp": x}


def merge_in_kernel(x_ref, gain_ref, shift_ref, w_ref, b_ref, o_ref, normed, joined):
    width = x_ref.shape[1]
    rows = x_ref.shape[0] // 4
    tiles = width // 128

    @pl.when(pl.program_id(0) == 0)
    def _():
        def body(i, carry):
            block = pl.ds(pl.multiple_of(i * 64, 64), 64)
            values = x_ref[block, :].astype(F32)
            center = values - jnp.mean(values, axis=-1, keepdims=True)
            spread = jnp.mean(center * center, axis=-1, keepdims=True)
            result = center * lax.rsqrt(spread + 1e-06) * gain_ref[...] + shift_ref[...]
            for u in range(tiles):
                normed[u, block, :] = result[:, u * 128 : (u + 1) * 128]
            return carry

        lax.fori_loop(0, x_ref.shape[0] // 64, body, 0)
        for t in range(4):
            for u in range(tiles):
                cols = slice((t * tiles + u) * 128, (t * tiles + u + 1) * 128)
                joined[:, cols] = normed[u, pl.ds(t, rows, stride=4), :].astype(BF16)

    total = jnp.dot(joined[...], w_ref[...], preferred_element_type=F32) + b_ref[...]
    o_ref[...] = (0.5 * total * (1.0 + lax.erf(total * (2.0**-0.5)))).astype(BF16)


def merge_in(patches, gain, shift, weight, bias):
    rows, width = patches.shape
    cols = weight.shape[1]
    step = 128
    return pl.pallas_call(
        merge_in_kernel,
        grid=(cols // step,),
        in_specs=[
            pl.BlockSpec((rows, width), lambda i: (0, 0)),
            pl.BlockSpec((1, width), lambda i: (0, 0)),
            pl.BlockSpec((1, width), lambda i: (0, 0)),
            pl.BlockSpec((4 * width, step), lambda i: (0, i)),
            pl.BlockSpec((1, step), lambda i: (0, i)),
        ],
        out_specs=pl.BlockSpec((rows // 4, step), lambda i: (0, i)),
        out_shape=jax.ShapeDtypeStruct((rows // 4, cols), BF16),
        scratch_shapes=[
            pltpu.VMEM((width // 128, rows, 128), F32),
            pltpu.VMEM((rows // 4, 4 * width), BF16),
        ],
        compiler_params=pltpu.CompilerParams(vmem_limit_bytes=40 * MIB),
        name="merge_in",
    )(
        patches,
        gain.astype(F32)[None, :],
        shift.astype(F32)[None, :],
        weight,
        bias.astype(F32)[None, :],
    )


def torus_gather_kernel(extra, x_ref, *refs):
    n_in = extra.n_in if extra else 0
    n_out = extra.n_out if extra else 0
    extra_in = refs[:n_in]
    out_ref = refs[n_in]
    extra_out = refs[n_in + 1 : n_in + 1 + n_out]
    a_send, a_recv, b_send, b_recv, s_send, s_recv, own_sem = refs[n_in + 1 + n_out : n_in + 8 + n_out]
    extra_sems = refs[n_in + 8 + n_out :]
    z, y, c, x = coords()
    half = x_ref.shape[0] // 2

    def chip(da, db, core):
        zz = lax.rem(z + da * (1 - core) + db * core + 8, 4)
        yy = lax.rem(y + da * core + db * (1 - core) + 8, 4)
        return zz, yy

    def where(da, db, core):
        zz, yy = chip(da, db, core)
        return place(zz, yy, core)

    def target(da, db):
        zz, yy = chip(da, db, c)
        return device(zz, yy, c, x)

    sibling = device(z, y, 1 - c, x)
    barrier = pltpu.get_barrier_semaphore()
    peers = [target(1, 0), target(-1, 0), target(0, 1), target(0, -1), sibling]
    if extra:
        peers = peers + extra.peers(z, y, c, x)
    for peer in peers:
        pl.semaphore_signal(barrier, inc=1, device_id=peer, device_id_type=MESH)
    pl.semaphore_wait(barrier, len(peers))

    started = []

    def view(da, db, core, part):
        s, q = where(da, db, core)
        if part is None:
            return out_ref.at[s, q]
        return out_ref.at[s, q, pl.ds(part * half, half)]

    def send(da, db, part, send_sem, recv_sem, to):
        source = view(da, db, c, part)
        if da == 0 and db == 0:
            source = x_ref
        copy = pltpu.make_async_remote_copy(
            src_ref=source,
            dst_ref=view(da, db, c, part),
            send_sem=send_sem,
            recv_sem=recv_sem,
            device_id=to,
            device_id_type=MESH,
        )
        copy.start()
        started.append(copy)

    def arrived(da, db, core, part, recv_sem, send_sem):
        block = view(da, db, core, part)
        pltpu.make_async_remote_copy(
            src_ref=block,
            dst_ref=block,
            send_sem=send_sem,
            recv_sem=recv_sem,
            device_id=sibling,
            device_id_type=MESH,
        ).wait_recv()

    def along_b(a, da):
        send(da, 0, None, b_send.at[a, 0], b_recv.at[a, 0], target(0, 1))
        send(da, 0, None, b_send.at[a, 1], b_recv.at[a, 1], target(0, -1))
        send(da, 0, None, s_send.at[a, 0], s_recv.at[a, 0], sibling)

    offsets = [0, -1, 1, 2]
    send(0, 0, None, a_send.at[0], a_recv.at[0], target(1, 0))
    send(0, 0, None, a_send.at[1], a_recv.at[1], target(-1, 0))
    along_b(0, 0)
    own_copy = pltpu.make_async_copy(x_ref, view(0, 0, c, None), own_sem)
    own_copy.start()
    if extra:
        extra_wait = extra.start(z, y, c, x, extra_in, extra_out, extra_sems)

    arrived(-1, 0, c, None, a_recv.at[0], a_send.at[0])
    send(-1, 0, 0, a_send.at[2], a_recv.at[2], target(1, 0))
    along_b(1, -1)
    arrived(1, 0, c, None, a_recv.at[1], a_send.at[1])
    send(1, 0, 1, a_send.at[3], a_recv.at[3], target(-1, 0))
    along_b(2, 1)

    def relay_b(a):
        da = offsets[a]
        arrived(da, -1, c, None, b_recv.at[a, 0], b_send.at[a, 0])
        send(da, -1, 0, b_send.at[a, 2], b_recv.at[a, 2], target(0, 1))
        send(da, -1, None, s_send.at[a, 1], s_recv.at[a, 1], sibling)
        arrived(da, 1, c, None, b_recv.at[a, 1], b_send.at[a, 1])
        send(da, 1, 1, b_send.at[a, 3], b_recv.at[a, 3], target(0, -1))
        send(da, 1, None, s_send.at[a, 2], s_recv.at[a, 2], sibling)

    relay_b(0)
    arrived(2, 0, c, 0, a_recv.at[2], a_send.at[2])
    arrived(2, 0, c, 1, a_recv.at[3], a_send.at[3])
    along_b(3, 2)
    for a in (1, 2, 3):
        relay_b(a)
    for a in range(4):
        da = offsets[a]
        arrived(da, 2, c, 0, b_recv.at[a, 2], b_send.at[a, 2])
        arrived(da, 2, c, 1, b_recv.at[a, 3], b_send.at[a, 3])
        send(da, 2, None, s_send.at[a, 3], s_recv.at[a, 3], sibling)
    for a in range(4):
        for b in range(4):
            arrived(offsets[a], offsets[b], 1 - c, None, s_recv.at[a, b], s_send.at[a, b])
    own_copy.wait()
    for copy in started:
        copy.wait_send()
    if extra:
        extra_wait()


def torus_gather(shard, collective_id, name, extra=None, operands=()):
    rows, cols = shard.shape
    dma = pltpu.SemaphoreType.DMA
    outs = [jax.ShapeDtypeStruct((2, 16, rows, cols), shard.dtype)]
    sems = [dma((4,)), dma((4,)), dma((4, 4)), dma((4, 4)), dma((4, 4)), dma((4, 4)), dma]
    if extra:
        outs = outs + extra.out_shapes
        sems = sems + extra.sems
    return pl.pallas_call(
        functools.partial(torus_gather_kernel, extra),
        out_shape=outs,
        in_specs=[ANY] * (1 + len(operands)),
        out_specs=[ANY] * len(outs),
        scratch_shapes=sems,
        compiler_params=pltpu.CompilerParams(collective_id=collective_id, has_side_effects=True),
        name=name,
    )(shard, *operands)


class Early:
    n_in = 2
    n_out = 2
    out_shapes = [
        jax.ShapeDtypeStruct((4, 96, 2048), BF16),
        jax.ShapeDtypeStruct((2, 640, 256), BF16),
    ]
    sems = [
        pltpu.SemaphoreType.DMA((4,)),
        pltpu.SemaphoreType.DMA((4,)),
        pltpu.SemaphoreType.DMA((2,)),
        pltpu.SemaphoreType.DMA((2,)),
    ]

    @staticmethod
    def peers(z, y, c, x):
        across = [device(z, y, c, lax.rem(x + d, 4)) for d in (1, 2, 3)]
        return across + [device(z, lax.rem(y + 2, 4), c, x)]

    @staticmethod
    def start(z, y, c, x, ins, outs, sems):
        text, weight = ins
        rows_out, weight_out = outs
        t_send, t_recv, w_send, w_recv = sems
        s = lax.div(y, 2)
        copies = []
        for d in (1, 2, 3):
            to = lax.rem(x + d, 4)
            copies.append(
                pltpu.make_async_remote_copy(
                    src_ref=text.at[pl.ds(pl.multiple_of(to * 96, 96), 96)],
                    dst_ref=rows_out.at[x],
                    send_sem=t_send.at[d],
                    recv_sem=t_recv.at[d],
                    device_id=device(z, y, c, to),
                    device_id_type=MESH,
                )
            )
        other = 1 - s
        copies.append(
            pltpu.make_async_remote_copy(
                src_ref=weight.at[:, pl.ds(pl.multiple_of(other * 256, 256), 256)],
                dst_ref=weight_out.at[s],
                send_sem=w_send.at[0],
                recv_sem=w_recv.at[0],
                device_id=device(z, lax.rem(y + 2, 4), c, x),
                device_id_type=MESH,
            )
        )
        copies.append(
            pltpu.make_async_copy(
                text.at[pl.ds(pl.multiple_of(x * 96, 96), 96)], rows_out.at[x], t_send.at[0]
            )
        )
        copies.append(
            pltpu.make_async_copy(
                weight.at[:, pl.ds(pl.multiple_of(s * 256, 256), 256)], weight_out.at[s], w_send.at[1]
            )
        )
        for copy in copies:
            copy.start()

        def wait():
            for d in (1, 2, 3):
                source = lax.rem(x + 4 - d, 4)
                pltpu.make_async_remote_copy(
                    src_ref=rows_out.at[source],
                    dst_ref=rows_out.at[source],
                    send_sem=t_send.at[d],
                    recv_sem=t_recv.at[d],
                    device_id=device(z, y, c, source),
                    device_id_type=MESH,
                ).wait_recv()
                copies[d - 1].wait_send()
            pltpu.make_async_remote_copy(
                src_ref=weight_out.at[other],
                dst_ref=weight_out.at[other],
                send_sem=w_send.at[0],
                recv_sem=w_recv.at[0],
                device_id=device(z, lax.rem(y + 2, 4), c, x),
                device_id_type=MESH,
            ).wait_recv()
            copies[3].wait_send()
            copies[4].wait()
            copies[5].wait()

        return wait


GROUP = 32


def merge_out_kernel(start_a, start_b, begin_b, h_ref, w_ref, o_ref, product):
    i = pl.program_id(0)
    total = jnp.dot(h_ref[0, 0], w_ref[0], preferred_element_type=F32)
    total = total + jnp.dot(h_ref[1, 0], w_ref[1], preferred_element_type=F32)
    for half in range(2):
        product[half, pl.ds(pl.multiple_of(i * 256, 256), 256), :] = total[:, half * 128 : (half + 1) * 128]

    @pl.when(i == pl.num_programs(0) - 1)
    def _():
        row = lax.broadcasted_iota(jnp.int32, (GROUP, 128), 0)

        def body(q, carry):
            for m in range(4):
                for k in range(3):
                    g = q * 12 + m * 3 + k
                    for half in range(2):
                        first = product[half, pl.ds(start_a[g], GROUP), :]
                        second = product[half, pl.ds(start_b[g], GROUP), :]
                        chosen = jnp.where(row >= begin_b[g], second, first).astype(BF16)
                        o_ref[m, k, q, :, half * 128 : (half + 1) * 128] = chosen
            return carry

        lax.fori_loop(0, 16, body, 0)


def merge_out(hidden, weight, start_a, start_b, begin_b):
    return pl.pallas_call(
        merge_out_kernel,
        grid_spec=pltpu.PrefetchScalarGridSpec(
            num_scalar_prefetch=3,
            grid=(16,),
            in_specs=[
                pl.BlockSpec((2, 1, 256, 640), lambda i, *_: (0, i, 0, 0)),
                pl.BlockSpec((2, 640, 256), lambda i, *_: (0, 0, 0)),
            ],
            out_specs=pl.BlockSpec((4, 3, 16, GROUP, 256), lambda i, *_: (0, 0, 0, 0, 0)),
            scratch_shapes=[pltpu.VMEM((2, 4096 + GROUP, 128), F32)],
        ),
        out_shape=jax.ShapeDtypeStruct((4, 3, 16, GROUP, 256), BF16),
        compiler_params=pltpu.CompilerParams(vmem_limit_bytes=40 * MIB),
        name="merge_out",
    )(start_a, start_b, begin_b, hidden, weight)


def spread_kernel(part, bias, text, visual_mask, out, summed, got, rows, r_send, r_recv, v_send, v_recv, own_sem, g_send, g_recv):
    z, y, c, x = coords()
    s, q = place(z, y, c)
    linear = s * 16 + q
    barrier = pltpu.get_barrier_semaphore()

    def peer(j):
        other = lax.rem(linear + j, 32)
        return lax.div(other, 16), lax.rem(other, 16)

    for d in (1, 2, 3):
        pl.semaphore_signal(
            barrier, inc=1, device_id=device(z, y, c, lax.rem(x + d, 4)), device_id_type=MESH
        )

    def greet(j, carry):
        ps, pq = peer(j)
        pl.semaphore_signal(
            barrier, inc=1, device_id={"section": ps, "seq": pq, "mp": x}, device_id_type=MESH
        )
        return carry

    lax.fori_loop(1, 32, greet, 0)
    pl.semaphore_wait(barrier, 34)

    def sum_copy(k, d):
        to = lax.rem(x + d, 4)
        return pltpu.make_async_remote_copy(
            src_ref=part.at[to, k],
            dst_ref=got.at[k, d - 1],
            send_sem=r_send.at[k, d - 1],
            recv_sem=r_recv.at[k, d - 1],
            device_id=device(z, y, c, to),
            device_id_type=MESH,
        )

    def start_sums(k):
        for d in (2, 1, 3):
            sum_copy(k, d).start()

    def add_up(k):
        for d in (1, 2, 3):
            sum_copy(k, d).wait_recv()

        def body(i, carry):
            total = part[x, k, i].astype(F32) + bias[...]
            for d in range(3):
                total = total + got[k, d, i].astype(F32)
            summed[k, i] = total.astype(BF16)
            return carry

        lax.fori_loop(0, 16, body, 0)

    def owner_copy(k, j):
        ps, pq = peer(j)
        return pltpu.make_async_remote_copy(
            src_ref=summed.at[k, pq],
            dst_ref=rows.at[k, q * 2 + s],
            send_sem=v_send.at[k],
            recv_sem=v_recv.at[k],
            device_id={"section": ps, "seq": pq, "mp": x},
            device_id_type=MESH,
        )

    def start_owner(k):
        def body(j, carry):
            owner_copy(k, j).start()
            return carry

        lax.fori_loop(1, 32, body, 0)
        pltpu.make_async_copy(summed.at[k, q], rows.at[k, q * 2 + s], own_sem.at[k]).start()

    def place_rows(k):
        pltpu.make_async_copy(summed.at[k, q], rows.at[k, q * 2 + s], own_sem.at[k]).wait()
        pltpu.make_async_copy(rows.at[k, pl.ds(0, 31)], rows.at[k, pl.ds(0, 31)], v_recv.at[k]).wait()
        visual = visual_mask[k * 32 : (k + 1) * 32, :] > 0.5
        for b in range(32):
            own_text = text[b // 8, k * 32 : (k + 1) * 32, (b % 8) * 256 : (b % 8 + 1) * 256]
            out[k, x, b] = jnp.where(visual, rows[k, b].astype(F32), own_text.astype(F32)).astype(BF16)

    def row_copy(k, part_index, origin, to, slot):
        if part_index is None:
            block = out.at[k, origin]
        else:
            block = out.at[k, origin, pl.ds(part_index * 16, 16)]
        return pltpu.make_async_remote_copy(
            src_ref=block,
            dst_ref=block,
            send_sem=g_send.at[k, slot],
            recv_sem=g_recv.at[k, slot],
            device_id=device(z, y, c, to),
            device_id_type=MESH,
        )

    right, left, across = lax.rem(x + 1, 4), lax.rem(x + 3, 4), lax.rem(x + 2, 4)

    def start_rows(k):
        row_copy(k, None, x, right, 0).start()
        row_copy(k, None, x, left, 1).start()

    def relay_rows(k):
        row_copy(k, None, left, right, 0).wait_recv()
        row_copy(k, 0, left, right, 2).start()
        row_copy(k, None, right, left, 1).wait_recv()
        row_copy(k, 1, right, left, 3).start()

    start_sums(0)
    start_sums(1)
    add_up(0)
    start_owner(0)
    start_sums(2)
    add_up(1)
    start_owner(1)
    place_rows(0)
    start_rows(0)
    add_up(2)
    start_owner(2)
    relay_rows(0)
    place_rows(1)
    start_rows(1)
    place_rows(2)
    start_rows(2)
    relay_rows(1)
    relay_rows(2)
    for k in range(3):
        row_copy(k, 0, across, right, 2).wait_recv()
        row_copy(k, 1, across, left, 3).wait_recv()
    for k in range(3):
        for d in (1, 2, 3):
            sum_copy(k, d).wait_send()
        pltpu.make_async_copy(rows.at[k, pl.ds(0, 31)], rows.at[k, pl.ds(0, 31)], v_send.at[k]).wait()
        row_copy(k, None, x, right, 0).wait_send()
        row_copy(k, None, x, left, 1).wait_send()
        row_copy(k, 0, left, right, 2).wait_send()
        row_copy(k, 1, right, left, 3).wait_send()


def spread(part, bias, text, visual_mask):
    dma = pltpu.SemaphoreType.DMA
    return pl.pallas_call(
        spread_kernel,
        out_shape=jax.ShapeDtypeStruct((3, 4, 32, GROUP, 256), BF16),
        in_specs=[VMEM] * 4,
        out_specs=VMEM,
        scratch_shapes=[
            pltpu.VMEM((3, 16, GROUP, 256), BF16),
            pltpu.VMEM((3, 3, 16, GROUP, 256), BF16),
            pltpu.VMEM((3, 32, GROUP, 256), BF16),
            dma((3, 3)),
            dma((3, 3)),
            dma((3,)),
            dma((3,)),
            dma((3,)),
            dma((3, 4)),
            dma((3, 4)),
        ],
        compiler_params=pltpu.CompilerParams(
            collective_id=2, has_side_effects=True, vmem_limit_bytes=48 * MIB
        ),
        name="spread",
    )(part, bias, text, visual_mask)


def project_kernel(x_ref, gain_ref, wq, wk, wv, bias, cos_ref, sin_ref, q_out, k_out, v_out, e_out, scale, total):
    i = pl.program_id(0)
    blocks = wq.shape[0] // 256
    order = [(k, m) for m in range(4) for k in range(3)]

    def rows_of(b):
        return jnp.concatenate([x_ref[k, m, b] for k, m in order], axis=0)

    @pl.when(i == 0)
    def _():
        def body(b, carry):
            values = rows_of(b).astype(F32)
            return carry + values * values

        squares = lax.fori_loop(0, 32, body, jnp.zeros((384, 256), F32))
        mean = jnp.sum(squares, axis=-1, keepdims=True) * (1.0 / 8192.0)
        scale[...] = jnp.broadcast_to(lax.rsqrt(mean + 1e-06), (384, 256))
        total[...] = jnp.broadcast_to(bias[...], total.shape)
        m0 = lax.axis_index("mp")
        for j in range(8):
            e_out[:, j * 256 : (j + 1) * 256] = rows_of(m0 * 8 + j)

    for j in range(blocks):
        b = i * blocks + j
        normed = (rows_of(b).astype(F32) * scale[...] * gain_ref[b]).astype(BF16)
        span = slice(j * 256, (j + 1) * 256)
        total[:, :512] += jnp.dot(normed, wq[span, :], preferred_element_type=F32)
        both = jnp.concatenate([wk[span, :], wv[span, :]], axis=1)
        total[:, 512:] += jnp.dot(normed, both, preferred_element_type=F32)

    @pl.when(i == pl.num_programs(0) - 1)
    def _():
        def rotate(values):
            return values * cos_ref[...] + pltpu.roll(values, 64, 1) * sin_ref[...]

        for h in range(4):
            cols = slice(h * 128, (h + 1) * 128)
            q_out[:, cols] = rotate(total[:, cols]).astype(BF16)
        k_out[...] = rotate(total[:, 512:640]).astype(BF16)
        v_out[...] = total[:, 640:].astype(BF16)


def project(x, gain, wq, wk, wv, bias, cos, sin):
    depth = 1024
    whole = lambda shape: pl.BlockSpec(shape, lambda i: (0,) * len(shape))
    return pl.pallas_call(
        project_kernel,
        grid=(8192 // depth,),
        in_specs=[
            whole(x.shape),
            whole((32, 1, 256)),
            pl.BlockSpec((depth, 512), lambda i: (i, 0)),
            pl.BlockSpec((depth, 128), lambda i: (i, 0)),
            pl.BlockSpec((depth, 128), lambda i: (i, 0)),
            whole((1, 768)),
            whole((384, 128)),
            whole((384, 128)),
        ],
        out_specs=[whole((384, 512)), whole((384, 128)), whole((384, 128)), whole((384, 2048))],
        out_shape=[
            jax.ShapeDtypeStruct((384, 512), BF16),
            jax.ShapeDtypeStruct((384, 128), BF16),
            jax.ShapeDtypeStruct((384, 128), BF16),
            jax.ShapeDtypeStruct((384, 2048), BF16),
        ],
        scratch_shapes=[pltpu.VMEM((384, 256), F32), pltpu.VMEM((384, 768), F32)],
        compiler_params=pltpu.CompilerParams(vmem_limit_bytes=48 * MIB),
        name="project",
    )(x, gain, wq, wk, wv, bias, cos, sin)


def attention_kernel(q_ref, kv_ref, o_ref, peak, norm, total):
    own = lax.axis_index("seq")
    rows = q_ref.shape[0]
    factor = HEAD**-0.5 * math.log2(math.e)
    peak[...] = jnp.full(peak.shape, -jnp.inf, F32)
    norm[...] = jnp.zeros(norm.shape, F32)
    total[...] = jnp.zeros(total.shape, F32)

    def block(j, masked):
        keys = kv_ref[0, j]
        values = kv_ref[1, j]
        for h in range(4):
            query = q_ref[:, h * HEAD : (h + 1) * HEAD]
            scores = lax.dot_general(
                query, keys, (((1,), (1,)), ((), ())), preferred_element_type=F32
            )
            if masked:
                row = lax.broadcasted_iota(jnp.int32, scores.shape, 0)
                col = lax.broadcasted_iota(jnp.int32, scores.shape, 1)
                scores = jnp.where(col <= row, scores, -jnp.inf)
            before = peak[h]
            after = jnp.maximum(before, jnp.max(scores, axis=1, keepdims=True))
            weights = jnp.exp2((scores - after[:, :1]) * factor)
            fade = jnp.exp2((before - after) * factor)
            peak[h] = after
            norm[h] = norm[h] * fade + jnp.sum(weights, axis=1, keepdims=True)
            total[h] = total[h] * fade + jnp.dot(
                weights.astype(BF16), values, preferred_element_type=F32
            )

    block(own, True)

    def body(j, carry):
        block(j, False)
        return carry

    lax.fori_loop(0, own, body, 0)
    for h in range(4):
        o_ref[:, h * HEAD : (h + 1) * HEAD] = (total[h] / norm[h]).astype(BF16)


def attention(queries, keys_values):
    rows = queries.shape[0]
    return pl.pallas_call(
        attention_kernel,
        out_shape=jax.ShapeDtypeStruct(queries.shape, BF16),
        in_specs=[VMEM, VMEM],
        out_specs=VMEM,
        scratch_shapes=[pltpu.VMEM((4, rows, HEAD), F32)] * 3,
        compiler_params=pltpu.CompilerParams(vmem_limit_bytes=40 * MIB),
        name="attention",
    )(queries, keys_values)


def local(
    patches,
    norm_gain,
    norm_shift,
    merge_in_weight,
    merge_in_bias,
    merge_out_weight,
    merge_out_bias,
    text_embeds,
    rms_gain,
    query_weight,
    query_bias,
    key_weight,
    key_bias,
    value_weight,
    value_bias,
    patch_counts,
    image_offsets,
):
    section = lax.axis_index("section")
    seq = lax.axis_index("seq")
    col = lax.axis_index("mp")
    own_rows = text_embeds.shape[0]
    tokens = patch_counts // 4
    first = jnp.arange(6144 // GROUP, dtype=jnp.int32) * GROUP
    image_a = jnp.sum((image_offsets[None, :] <= first[:, None]).astype(jnp.int32), axis=1) - 1
    image_b = jnp.minimum(image_a + 1, 15)
    pick_a = image_a[:, None] == jnp.arange(16, dtype=jnp.int32)[None, :]
    pick_b = image_b[:, None] == jnp.arange(16, dtype=jnp.int32)[None, :]
    offset_a = jnp.sum(jnp.where(pick_a, image_offsets[None, :], 0), axis=1)
    offset_b = jnp.sum(jnp.where(pick_b, image_offsets[None, :], 0), axis=1)
    begin_b = jnp.where(image_a == 15, GROUP, jnp.minimum(offset_b - first, GROUP))
    start_a = jnp.minimum(image_a * 256 + first - offset_a, 4096)
    start_b = image_b * 256 - begin_b
    own_positions = seq * own_rows + jnp.arange(own_rows, dtype=jnp.int32)
    block_positions = seq * own_rows + col * 96 + jnp.arange(96, dtype=jnp.int32)
    relative = block_positions[:, None] - image_offsets[None, :]
    is_visual = jnp.any((relative >= 0) & (relative < tokens[None, :]), axis=1)
    visual_mask = jnp.broadcast_to(is_visual[:, None].astype(F32), (96, 256))
    half_dim = HEAD // 2
    inv_freq = jnp.exp(jnp.arange(half_dim, dtype=F32) * (-2.0 * math.log(1000000.0) / HEAD))
    angles = own_positions.astype(F32)[:, None] * inv_freq[None, :]
    cosine, sine = jnp.cos(angles), jnp.sin(angles)
    cos_table = jnp.concatenate([cosine, cosine], axis=1)
    sin_table = jnp.concatenate([-sine, sine], axis=1)

    hidden = merge_in(patches, norm_gain, norm_shift, merge_in_weight, merge_in_bias)
    all_hidden, text_rows, out_weight = torus_gather(
        hidden, 0, "gather_hidden", Early, (text_embeds, merge_out_weight)
    )
    part = merge_out(all_hidden, out_weight, start_a, start_b, begin_b)
    out_bias = lax.dynamic_slice_in_dim(merge_out_bias, section * 256, 256, 0).astype(F32)[None, :]
    rows = spread(part, out_bias, text_rows, visual_mask)
    bias = jnp.concatenate([query_bias, key_bias, value_bias]).astype(F32)[None, :]
    gain = rms_gain.astype(F32).reshape(32, 1, 256)
    queries, keys, values, embeds = project(
        rows, gain, query_weight, key_weight, value_weight, bias, cos_table, sin_table
    )
    shared = jnp.where(section == 0, keys, values)
    (keys_values,) = torus_gather(shared, 1, "gather_keys")
    return (embeds, attention(queries, keys_values))


def solution(mesh):
    placed = (
        P("seq", None),
        P(),
        P(),
        P(None, ("section", "mp")),
        P(("section", "mp")),
        P(("section", "mp"), "seq"),
        P("seq"),
        P("seq", "mp"),
        P(),
        P(None, ("section", "mp")),
        P(("section", "mp")),
        P(None, "mp"),
        P("mp"),
        P(None, "mp"),
        P("mp"),
        P(),
        P(),
    )
    return jax.shard_map(
        local,
        mesh=mesh,
        in_specs=placed,
        out_specs=(P("seq", "mp"), P("seq", ("section", "mp"))),
        check_vma=False,
    )
```

time: 790 us -> 249 us (0.32)
  waiting for transfers between devices: 256 us -> 0 us
  blocking collectives: 252 us -> 0 us
  Pallas kernels: 0 us -> 229 us
  other arithmetic: 111 us -> 3.32 us
  matrix products: 67.6 us -> 0 us
  local copies, waits for them, and re-layouts: 77.6 us -> 15.9 us
  between operations: 14 us -> 0.87 us
    psum x1 -> x0, blocking collectives: 252 us -> none  [local(): visual = lax.psum(routed, ('section', 'mp')).astype(jnp.bfloat16)]
    pallas_call x0 -> x7, Pallas kernels: none -> 229 us  [the longest x1 93.4 us: spread(): pl.pallas_call(spread_kernel, out_shape=jax.ShapeDtypeStruct((3, 4, 32, G...]
    all_to_all x1 -> x0, waiting for transfers between devices: 136 us -> none  [local(): lax.all_to_all(partial_value, 'seq', split_axis=0, concat_axis=1, tiled=T...]
    all_gather x4 -> x0, waiting for transfers between devices: 120 us -> none  [the longest x1 66.8 us: local(): whole_rows = lax.all_gather(embeds, 'mp', axis=1, tiled=True)]
    sub x1, other arithmetic: 88.2 us -> 0.01 us  [local(): jnp.sum((image_offsets[None, :] <= first[:, None]).astype(jnp.int32), axi...]
    dot_general x7 -> x0, matrix products: 67.6 us -> none  [the longest x3 19.2 us: project(): jnp.dot(normed_seq, weight, preferred_element_type=jnp.float32)]
    gather x1 -> x0, local copies, waits for them, and re-layouts: 29.7 us -> none  [local(): jnp.take(gathered, slot_rows, axis=0)]
    broadcast_in_dim x2 -> x4, local copies, waits for them, and re-layouts: 17.1 us -> 2.14 us  [the longest x1 0.69 us: merge_in(): gain.astype(F32)[None, :]]
  transfers between devices with their start and end apart: 5 -> 0, of which waited for: 4 -> 0; matrix products, arithmetic and copies ran while one was open for 20% -> 0% of each run, Pallas kernels for 0% -> 0%
where the time goes in v1:
time: 249 us
  Pallas kernels  229 us (92%)
  local copies, waits for them, and re-layouts  15.9 us (6%)
  other arithmetic  3.32 us (1%)
    pallas_call x1, Pallas kernels, spread(): pl.pallas_call(spread_kernel, out_shape=jax.ShapeDtypeStruct((3, 4, 32, G...  93.4 us
    pallas_call x2, Pallas kernels, torus_gather(): pl.pallas_call(functools.partial(torus_gather_kernel, extra), out_shape=o...  63.7 us
    pallas_call x1, Pallas kernels, attention(): pl.pallas_call(attention_kernel, out_shape=jax.ShapeDtypeStruct(queries.s...  37.1 us
    pallas_call x1, Pallas kernels, project(): pl.pallas_call(project_kernel, grid=(8192 // depth,), in_specs=[whole(x.s...  16.1 us
    unnamed x32, local copies, waits for them, and re-layouts  13.7 us
    pallas_call x1, Pallas kernels, merge_in(): pl.pallas_call(merge_in_kernel, grid=(cols // step,), in_specs=[pl.BlockS...  9.87 us
    pallas_call x1, Pallas kernels, merge_out(): pl.pallas_call(merge_out_kernel, grid_spec=pltpu.PrefetchScalarGridSpec(n...  8.49 us

profile of v1, /device:TPU:105, one launch (start us, length us, event | category | flops | bytes accessed | tf_op | source)
XLA Modules:
  0.0 248.7 jit_solution(15649180335064279616)
XLA Ops:
  0.6 0.7 convert_reduce_fusion
  1.4 0.7 select_reduce_fusion
  2.2 0.7 reshape.84.gain_ref
  2.8 0.7 reshape.85.shift_ref
  3.5 0.7 reshape.86.b_ref
  4.2 0.0 copy-start.2
  4.2 2.9 %copy-done.2 = bf16[5120,640]{1,0:T(8,128)(2,1)S(1)} copy-done((bf16[5120,640]{1,0:T(8,128)(2,1)S(1)}, bf16[5120,640]{1,0:T(8,128)(2,1)}, u32[]{:S(2)}) %copy-start.2) | copy-done | bytes 6553624
  7.1 0.0 copy-start.3
  7.1 1.7 copy-done.3
  8.8 9.9 %merge_in.1.x_ref = bf16[256,640]{1,0:T(8,128)(2,1)S(1)} custom-call(bf16[1024,1280]{1,0:T(8,128)(2,1)S(1)} %copy-done.3, f32[1,1280]{1,0:T(1,128)S(1)} %reshape.84.gain_ref, f32[1,1280]{1,0:T(1,128)S(1)} %reshape.85.shift_ref, bf16[5120,640]{1,0:T(8,128)(2,1)S(1)} %copy-done.2, f32[1,640]{1,0:T(1,128)S(1)} %reshape.86.b_ref), custom_call_target="tpu_custom_call" | custom-call | tf_op jit(solution)/shard_map/merge_in/pallas_call | solution.py:68
  18.7 0.0 copy-start.7
  18.7 0.7 copy-done.7
  19.4 42.1 %gather_hidden.1 = (bf16[2,16,256,640]{3,2,1,0:T(8,128)(2,1)}, bf16[4,96,2048]{2,1,0:T(8,128)(2,1)}, bf16[2,640,256]{2,1,0:T(8,128)(2,1)}) custom-call(bf16[256,640]{1,0:T(8,128)(2,1)} %copy-done.7, bf16[384,2048]{1,0:T(8,128)(2,1)} %refs_0_.1, bf16[640,512]{1,0:T(8,128)(2,1)} %refs_1_.1), custom_call_target="tpu_custom_call" | custom-call | tf_op jit(solution)/shard_map/gather_hidden/pallas_call | solution.py:221
  61.5 0.0 copy-start.1
  61.5 4.0 %copy-done.1 = bf16[2,16,256,640]{3,2,1,0:T(8,128)(2,1)S(1)} copy-done((bf16[2,16,256,640]{3,2,1,0:T(8,128)(2,1)S(1)}, bf16[2,16,256,640]{3,2,1,0:T(8,128)(2,1)}, u32[]{:S(2)}) %copy-start.1) | copy-done | bytes 10485784
  65.5 0.0 copy-start.8
  65.5 1.1 copy-done.8
  66.6 0.0 copy-start.14
  66.6 0.0 copy-start.15
  66.6 0.0 copy-start.10
  66.6 8.5 %merge_out.1.part = bf16[4,3,16,32,256]{4,3,2,1,0:T(8,128)(2,1)S(1)} custom-call(s32[192]{0:T(256)S(1)} %get-tuple-element.23.start_a, s32[192]{0:T(256)S(1)} %get-tuple-element.22.start_b, s32[192]{0:T(256)S(1)} %get-tuple-element.21.begin_b, bf16[2,16,256,640]{3,2,1,0:T(8,128)(2,1)S(1)} %copy-done.1, bf16[2,640,256]{2,1,0:T(8,128)(2,1)S(1)} %copy-done.8), custom_call_target="tpu_custom_call" | custom-call | tf_op jit(solution)/shard_map/merge_out/pallas_call | solution.py:350
  75.1 0.0 copy-done.14
  75.1 0.1 dynamic-slice_convert_fusion
  75.2 0.0 copy-done.15
  75.2 0.0 copy-done.10
  75.2 0.1 fusion.2
  75.3 0.1 broadcast_in_dim.65.visual_mask
  75.4 0.0 copy-start.6
  75.4 1.4 copy-done.6
  76.8 0.0 copy-start.9
  76.8 0.0 copy-start.11
  76.8 0.0 copy-start.4
  76.8 0.0 copy-start.5
  76.8 93.4 %spread.1.x_ref = bf16[3,4,32,32,256]{4,3,2,1,0:T(8,128)(2,1)} custom-call(bf16[4,3,16,32,256]{4,3,2,1,0:T(8,128)(2,1)S(1)} %merge_out.1.part, f32[1,256]{1,0:T(1,128)S(1)} %bitcast.5, bf16[4,96,2048]{2,1,0:T(8,128)(2,1)S(1)} %copy-done.6, f32[96,256]{1,0:T(8,128)S(1)} %broadcast_in_dim.65.visual_mask), custom_call_target="tpu_custom_call" | custom-call | tf_op jit(solution)/shard_map/spread/pallas_call | solution.py:507
  170.3 0.8 fusion
  171.1 0.2 pad_maximum_fusion
  171.3 0.0 copy-done.9
  171.3 0.0 copy-done.11
  171.3 0.0 copy-done.12
  171.3 0.0 copy-done.13
  171.4 0.0 copy-done.4
  171.4 0.0 copy-done.5
  171.4 16.1 %project.1 = (bf16[384,512]{1,0:T(8,128)(2,1)S(1)}, bf16[384,128]{1,0:T(8,128)(2,1)S(1)}, bf16[384,128]{1,0:T(8,128)(2,1)S(1)}, bf16[384,2048]{1,0:T(8,128)(2,1)}) custom-call(bf16[3,4,32,32,256]{4,3,2,1,0:T(8,128)(2,1)} %spread.1.x_ref, f32[32,1,256]{2,1,0:T(1,128)S(1)} %bitcast.4, bf16[8192,512]{1,0:T(8,128)(2,1)} %wq.1, bf16[8192,128]{1,0:T(8,128)(2,1)S(1)} %copy-done.4, ...), custom_call_target="tpu_custom_call" | custom-call | tf_op jit(solution)/shard_map/project/pallas_call | solution.py:576
  187.5 0.7 broadcast_select_fusion.x_ref
  188.1 21.6 %gather_keys.1.kv_ref = bf16[2,16,384,128]{3,2,1,0:T(8,128)(2,1)} custom-call(bf16[384,128]{1,0:T(8,128)(2,1)} %broadcast_select_fusion.x_ref), custom_call_target="tpu_custom_call" | custom-call | tf_op jit(solution)/shard_map/gather_keys/pallas_call | solution.py:221
  209.7 0.0 copy-start
  209.7 1.9 copy-done
  211.6 37.1 %attention.1 = bf16[384,512]{1,0:T(8,128)(2,1)} custom-call(bf16[384,512]{1,0:T(8,128)(2,1)S(1)} %get-tuple-element.13.q_ref, bf16[2,16,384,128]{3,2,1,0:T(8,128)(2,1)S(1)} %copy-done), custom_call_target="tpu_custom_call" | custom-call | tf_op jit(solution)/shard_map/attention/pallas_call | solution.py:645
  (13 shorter events, 0.1 us)
Async XLA Ops:
  4.2 2.9 %copy-start.2 = (bf16[5120,640]{1,0:T(8,128)(2,1)S(1)}, bf16[5120,640]{1,0:T(8,128)(2,1)}, u32[]{:S(2)}) copy-start(bf16[5120,640]{1,0:T(8,128)(2,1)} %w_ref.1) | copy-start | bytes 19660804
  7.1 1.7 copy-start.3
  18.7 0.7 copy-start.7
  61.5 4.0 %copy-start.1 = (bf16[2,16,256,640]{3,2,1,0:T(8,128)(2,1)S(1)}, bf16[2,16,256,640]{3,2,1,0:T(8,128)(2,1)}, u32[]{:S(2)}) copy-start(bf16[2,16,256,640]{3,2,1,0:T(8,128)(2,1)} %get-tuple-element.9.h_ref) | copy-start | bytes 31457284
  65.5 1.1 copy-start.8
  66.6 8.5 %copy-start.14 = (bf16[512]{0:T(512)(128)(2,1)S(1)}, bf16[512]{0:T(512)(128)(2,1)}, u32[]{:S(2)}) copy-start(bf16[512]{0:T(512)(128)(2,1)} %param.23) | copy-start | bytes 3076
  66.6 8.6 %copy-start.15 = (s32[16]{0:T(128)S(1)}, s32[16]{0:T(128)}, u32[]{:S(2)}) copy-start(s32[16]{0:T(128)} %param.32) | copy-start | bytes 196
  66.6 8.6 %copy-start.10 = (s32[16]{0:T(128)S(1)}, s32[16]{0:T(128)}, u32[]{:S(2)}) copy-start(s32[16]{0:T(128)} %param.33) | copy-start | bytes 196
  75.4 1.4 copy-start.6
  76.8 94.5 %copy-start.9 = (bf16[8192]{0:T(1024)(128)(2,1)S(1)}, bf16[8192]{0:T(1024)(128)(2,1)}, u32[]{:S(2)}) copy-start(bf16[8192]{0:T(1024)(128)(2,1)} %param.25) | copy-start | bytes 49156
  76.8 94.5 %copy-start.11 = (bf16[512]{0:T(512)(128)(2,1)S(1)}, bf16[512]{0:T(512)(128)(2,1)}, u32[]{:S(2)}) copy-start(bf16[512]{0:T(512)(128)(2,1)} %param.27) | copy-start | bytes 3076
  76.8 94.5 %copy-start.12 = (bf16[128]{0:T(256)(128)(2,1)S(1)}, bf16[128]{0:T(256)(128)(2,1)}, u32[]{:S(2)}) copy-start(bf16[128]{0:T(256)(128)(2,1)} %param.31) | copy-start | bytes 772
  76.8 94.5 %copy-start.13 = (bf16[128]{0:T(256)(128)(2,1)S(1)}, bf16[128]{0:T(256)(128)(2,1)}, u32[]{:S(2)}) copy-start(bf16[128]{0:T(256)(128)(2,1)} %param.29) | copy-start | bytes 772
  76.8 94.5 %copy-start.4 = (bf16[8192,128]{1,0:T(8,128)(2,1)S(1)}, bf16[8192,128]{1,0:T(8,128)(2,1)}, u32[]{:S(2)}) copy-start(bf16[8192,128]{1,0:T(8,128)(2,1)} %wk.1) | copy-start | bytes 6291460
  76.8 94.5 %copy-start.5 = (bf16[8192,128]{1,0:T(8,128)(2,1)S(1)}, bf16[8192,128]{1,0:T(8,128)(2,1)}, u32[]{:S(2)}) copy-start(bf16[8192,128]{1,0:T(8,128)(2,1)} %wv.1) | copy-start | bytes 6291460
  209.7 1.9 copy-start

commit v2 on v0

v2 whole, which is shorter than its diff:
```python
import math

import jax
import jax.numpy as jnp
from jax import lax
from jax.experimental import pallas as pl
from jax.experimental.pallas import tpu as pltpu
from jax.sharding import PartitionSpec as P

HEAD = 128
MESH = pl.DeviceIdType.MESH
MIB = 1024 * 1024
ANY = pl.BlockSpec(memory_space=pl.ANY)
VMEM = pl.BlockSpec(memory_space=pltpu.VMEM)
BF16 = jnp.bfloat16
F32 = jnp.float32


def coords():
    s = lax.axis_index("section")
    q = lax.axis_index("seq")
    z = lax.div(q, 4)
    y = s * 2 + lax.rem(lax.div(q, 2), 2)
    return z, y, lax.rem(q, 2), lax.axis_index("mp")


def place(z, y, c):
    return lax.div(y, 2), z * 4 + lax.rem(y, 2) * 2 + c


def device(z, y, c, x):
    s, q = place(z, y, c)
    return {"section": s, "seq": q, "mp": x}


def merge_in_kernel(x_ref, gain_ref, shift_ref, w_ref, b_ref, o_ref, normed, joined):
    width = x_ref.shape[1]
    rows = x_ref.shape[0] // 4
    tiles = width // 128

    @pl.when(pl.program_id(0) == 0)
    def _():
        def body(i, carry):
            block = pl.ds(pl.multiple_of(i * 64, 64), 64)
            values = x_ref[block, :].astype(F32)
            center = values - jnp.mean(values, axis=-1, keepdims=True)
            spread = jnp.mean(center * center, axis=-1, keepdims=True)
            result = center * lax.rsqrt(spread + 1e-06) * gain_ref[...] + shift_ref[...]
            for u in range(tiles):
                normed[u, block, :] = result[:, u * 128 : (u + 1) * 128]
            return carry

        lax.fori_loop(0, x_ref.shape[0] // 64, body, 0)
        for t in range(4):
            for u in range(tiles):
                cols = slice((t * tiles + u) * 128, (t * tiles + u + 1) * 128)
                joined[:, cols] = normed[u, pl.ds(t, rows, stride=4), :].astype(BF16)

    total = jnp.dot(joined[...], w_ref[...], preferred_element_type=F32) + b_ref[...]
    o_ref[...] = (0.5 * total * (1.0 + lax.erf(total * (2.0**-0.5)))).astype(BF16)


def merge_in(patches, gain, shift, weight, bias):
    rows, width = patches.shape
    cols = weight.shape[1]
    step = 128
    return pl.pallas_call(
        merge_in_kernel,
        grid=(cols // step,),
        in_specs=[
            pl.BlockSpec((rows, width), lambda i: (0, 0)),
            pl.BlockSpec((1, width), lambda i: (0, 0)),
            pl.BlockSpec((1, width), lambda i: (0, 0)),
            pl.BlockSpec((4 * width, step), lambda i: (0, i)),
            pl.BlockSpec((1, step), lambda i: (0, i)),
        ],
        out_specs=pl.BlockSpec((rows // 4, step), lambda i: (0, i)),
        out_shape=jax.ShapeDtypeStruct((rows // 4, cols), BF16),
        scratch_shapes=[
            pltpu.VMEM((width // 128, rows, 128), F32),
            pltpu.VMEM((rows // 4, 4 * width), BF16),
        ],
        compiler_params=pltpu.CompilerParams(vmem_limit_bytes=60 * MIB),
        name="merge_in",
    )(
        patches,
        gain.astype(F32)[None, :],
        shift.astype(F32)[None, :],
        weight,
        bias.astype(F32)[None, :],
    )


def torus_sems():
    dma = pltpu.SemaphoreType.DMA
    return [dma((4,)), dma((4,)), dma((4, 4)), dma((4, 4)), dma((4, 4)), dma((4, 4)), dma]


class Torus:
    def __init__(self, x_ref, out_ref, sems):
        self.x_ref, self.out_ref = x_ref, out_ref
        self.a_send, self.a_recv, self.b_send, self.b_recv, self.s_send, self.s_recv, self.own_sem = sems
        self.z, self.y, self.c, self.x = coords()
        self.half = x_ref.shape[0] // 2
        self.started = []
        self.sibling = device(self.z, self.y, 1 - self.c, self.x)

    def where(self, da, db, core):
        zz = lax.rem(self.z + da * (1 - core) + db * core + 8, 4)
        yy = lax.rem(self.y + da * core + db * (1 - core) + 8, 4)
        return place(zz, yy, core)

    def target(self, da, db):
        s, q = self.where(da, db, self.c)
        return {"section": s, "seq": q, "mp": self.x}

    def peers(self):
        return [self.target(1, 0), self.target(-1, 0), self.target(0, 1), self.target(0, -1), self.sibling]

    def view(self, da, db, core, part):
        s, q = self.where(da, db, core)
        if part is None:
            return self.out_ref.at[s, q]
        return self.out_ref.at[s, q, pl.ds(part * self.half, self.half)]

    def send(self, da, db, part, send_sem, recv_sem, to):
        block = self.view(da, db, self.c, part)
        copy = pltpu.make_async_remote_copy(
            src_ref=self.x_ref if da == 0 and db == 0 else block,
            dst_ref=block,
            send_sem=send_sem,
            recv_sem=recv_sem,
            device_id=to,
            device_id_type=MESH,
        )
        copy.start()
        self.started.append(copy)

    def arrived(self, da, db, core, part, send_sem, recv_sem):
        block = self.view(da, db, core, part)
        pltpu.make_async_remote_copy(
            src_ref=block,
            dst_ref=block,
            send_sem=send_sem,
            recv_sem=recv_sem,
            device_id=self.sibling,
            device_id_type=MESH,
        ).wait_recv()

    def along_b(self, a, da):
        self.send(da, 0, None, self.b_send.at[a, 0], self.b_recv.at[a, 0], self.target(0, 1))
        self.send(da, 0, None, self.b_send.at[a, 1], self.b_recv.at[a, 1], self.target(0, -1))
        self.send(da, 0, None, self.s_send.at[a, 0], self.s_recv.at[a, 0], self.sibling)

    def start(self):
        self.send(0, 0, None, self.a_send.at[0], self.a_recv.at[0], self.target(1, 0))
        self.send(0, 0, None, self.a_send.at[1], self.a_recv.at[1], self.target(-1, 0))
        self.along_b(0, 0)
        self.own_copy = pltpu.make_async_copy(self.x_ref, self.view(0, 0, self.c, None), self.own_sem)
        self.own_copy.start()

    def run(self, use):
        offsets = [0, -1, 1, 2]
        c = self.c

        def from_sibling(a, b):
            da, db = offsets[a], offsets[b]
            self.arrived(da, db, 1 - c, None, self.s_send.at[a, b], self.s_recv.at[a, b])
            use(*self.where(da, db, 1 - c))

        def relay_b(a):
            da = offsets[a]
            self.arrived(da, -1, c, None, self.b_send.at[a, 0], self.b_recv.at[a, 0])
            self.send(da, -1, 0, self.b_send.at[a, 2], self.b_recv.at[a, 2], self.target(0, 1))
            self.send(da, -1, None, self.s_send.at[a, 1], self.s_recv.at[a, 1], self.sibling)
            self.arrived(da, 1, c, None, self.b_send.at[a, 1], self.b_recv.at[a, 1])
            self.send(da, 1, 1, self.b_send.at[a, 3], self.b_recv.at[a, 3], self.target(0, -1))
            self.send(da, 1, None, self.s_send.at[a, 2], self.s_recv.at[a, 2], self.sibling)
            use(*self.where(da, -1, c))
            use(*self.where(da, 1, c))

        self.own_copy.wait()
        use(*self.where(0, 0, c))
        self.arrived(-1, 0, c, None, self.a_send.at[0], self.a_recv.at[0])
        self.send(-1, 0, 0, self.a_send.at[2], self.a_recv.at[2], self.target(1, 0))
        self.along_b(1, -1)
        self.arrived(1, 0, c, None, self.a_send.at[1], self.a_recv.at[1])
        self.send(1, 0, 1, self.a_send.at[3], self.a_recv.at[3], self.target(-1, 0))
        self.along_b(2, 1)
        use(*self.where(-1, 0, c))
        use(*self.where(1, 0, c))
        from_sibling(0, 0)
        relay_b(0)
        self.arrived(2, 0, c, 0, self.a_send.at[2], self.a_recv.at[2])
        self.arrived(2, 0, c, 1, self.a_send.at[3], self.a_recv.at[3])
        self.along_b(3, 2)
        use(*self.where(2, 0, c))
        from_sibling(1, 0)
        from_sibling(2, 0)
        for a in (1, 2, 3):
            relay_b(a)
            from_sibling(a - 1, 1)
            from_sibling(a - 1, 2)
        from_sibling(3, 0)
        from_sibling(3, 1)
        from_sibling(3, 2)
        for a in range(4):
            da = offsets[a]
            self.arrived(da, 2, c, 0, self.b_send.at[a, 2], self.b_recv.at[a, 2])
            self.arrived(da, 2, c, 1, self.b_send.at[a, 3], self.b_recv.at[a, 3])
            self.send(da, 2, None, self.s_send.at[a, 3], self.s_recv.at[a, 3], self.sibling)
            use(*self.where(da, 2, c))
        for a in range(4):
            from_sibling(a, 3)

    def finish(self):
        for copy in self.started:
            copy.wait_send()


def greet(peers):
    barrier = pltpu.get_barrier_semaphore()
    for peer in peers:
        pl.semaphore_signal(barrier, inc=1, device_id=peer, device_id_type=MESH)
    pl.semaphore_wait(barrier, len(peers))


GROUP = 32


def merge_out_kernel(
    start_a, start_b, begin_b, x_ref, w_own, w_other, text, o_ref, text_rows, hidden, weight, product, t_send, t_recv, w_sem, *sems
):
    torus = Torus(x_ref, hidden, sems)
    z, y, c, x = coords()
    greet(torus.peers() + [device(z, y, c, lax.rem(x + d, 4)) for d in (1, 2, 3)])
    torus.start()
    loads = [
        pltpu.make_async_copy(w_own, weight.at[0], w_sem.at[0]),
        pltpu.make_async_copy(w_other, weight.at[1], w_sem.at[1]),
        pltpu.make_async_copy(text.at[pl.ds(pl.multiple_of(x * 96, 96), 96)], text_rows.at[x], t_send.at[0]),
    ]
    for load in loads:
        load.start()

    def text_copy(d):
        to = lax.rem(x + d, 4)
        return pltpu.make_async_remote_copy(
            src_ref=text.at[pl.ds(pl.multiple_of(to * 96, 96), 96)],
            dst_ref=text_rows.at[x],
            send_sem=t_send.at[d],
            recv_sem=t_recv.at[d],
            device_id=device(z, y, c, to),
            device_id_type=MESH,
        )

    for d in (1, 2, 3):
        text_copy(d).start()
    product[...] = jnp.zeros(product.shape, F32)
    loads[0].wait()
    loads[1].wait()
    own_section = lax.div(y, 2)

    def use(s, q):
        total = jnp.dot(hidden[s, q], weight[lax.rem(s + own_section, 2)], preferred_element_type=F32)
        rows = pl.ds(pl.multiple_of(q * 256, 256), 256)
        for half in range(2):
            product[half, rows, :] += total[:, half * 128 : (half + 1) * 128]

    torus.run(use)
    row = lax.broadcasted_iota(jnp.int32, (GROUP, 128), 0)

    def body(q, carry):
        for m in range(4):
            for k in range(3):
                g = q * 12 + m * 3 + k
                for half in range(2):
                    first = product[half, pl.ds(start_a[g], GROUP), :]
                    second = product[half, pl.ds(start_b[g], GROUP), :]
                    chosen = jnp.where(row >= begin_b[g], second, first).astype(BF16)
                    o_ref[m, k, q, :, half * 128 : (half + 1) * 128] = chosen
        return carry

    lax.fori_loop(0, 16, body, 0)
    torus.finish()
    loads[2].wait()
    for d in (1, 2, 3):
        source = lax.rem(x + 4 - d, 4)
        pltpu.make_async_remote_copy(
            src_ref=text_rows.at[source],
            dst_ref=text_rows.at[source],
            send_sem=t_send.at[d],
            recv_sem=t_recv.at[d],
            device_id=device(z, y, c, source),
            device_id_type=MESH,
        ).wait_recv()
        text_copy(d).wait_send()


def merge_out(hidden, w_own, w_other, text, start_a, start_b, begin_b):
    dma = pltpu.SemaphoreType.DMA
    smem = pl.BlockSpec(memory_space=pltpu.SMEM)
    return pl.pallas_call(
        merge_out_kernel,
        in_specs=[smem, smem, smem, VMEM, ANY, ANY, ANY],
        out_specs=[VMEM, ANY],
        out_shape=[
            jax.ShapeDtypeStruct((4, 3, 16, GROUP, 256), BF16),
            jax.ShapeDtypeStruct((4, 96, 2048), BF16),
        ],
        scratch_shapes=[
            pltpu.VMEM((2, 16, 256, 640), BF16),
            pltpu.VMEM((2, 640, 256), BF16),
            pltpu.VMEM((2, 4096 + GROUP, 128), F32),
            dma((4,)),
            dma((4,)),
            dma((2,)),
        ]
        + torus_sems(),
        compiler_params=pltpu.CompilerParams(
            collective_id=0, has_side_effects=True, vmem_limit_bytes=60 * MIB
        ),
        name="merge_out",
    )(start_a, start_b, begin_b, hidden, w_own, w_other, text)


def spread_kernel(
    part, out_bias, visual_mask, gain, bias, cos_ref, sin_ref, text_ref, wq_ref, wk_ref, wv_ref,
    q_out, kv_out, e_out,
    relay, relayed, got, summed, rows, text, out, normed, wq, wkv, total,
    r_send, r_recv, v_send, v_recv, own_sem, g_send, g_recv, load_sem,
):
    z, y, c, x = coords()
    s, q = place(z, y, c)
    linear = s * 16 + q
    right, left, across = lax.rem(x + 1, 4), lax.rem(x + 3, 4), lax.rem(x + 2, 4)
    to_right, to_left = device(z, y, c, right), device(z, y, c, left)
    pltpu.make_async_copy(text_ref, text, load_sem.at[0]).start()
    pltpu.make_async_copy(wq_ref, wq, load_sem.at[1]).start()

    @pl.when(s == 0)
    def _():
        pltpu.make_async_copy(wk_ref, wkv, load_sem.at[2]).start()

    @pl.when(s == 1)
    def _():
        pltpu.make_async_copy(wv_ref, wkv, load_sem.at[2]).start()

    def peer(j):
        other = lax.rem(linear + j, 32)
        return lax.div(other, 16), lax.rem(other, 16)

    barrier = pltpu.get_barrier_semaphore()
    for to in (to_right, to_left):
        pl.semaphore_signal(barrier, inc=1, device_id=to, device_id_type=MESH)

    def hello(j, carry):
        ps, pq = peer(j)
        pl.semaphore_signal(
            barrier, inc=1, device_id={"section": ps, "seq": pq, "mp": x}, device_id_type=MESH
        )
        return carry

    lax.fori_loop(1, 32, hello, 0)
    pl.semaphore_wait(barrier, 33)

    TOP, BOTTOM = pl.ds(0, 8), pl.ds(8, 8)

    def sum_copy(k, i):
        source, target, to = [
            (part.at[across, k, TOP], relay.at[k, 0], to_right),
            (part.at[across, k, BOTTOM], relay.at[k, 1], to_left),
            (part.at[right, k, BOTTOM], got.at[k, 0, BOTTOM], to_right),
            (part.at[left, k, TOP], got.at[k, 1, TOP], to_left),
            (relayed.at[k, 0], got.at[k, 0, TOP], to_right),
            (relayed.at[k, 1], got.at[k, 1, BOTTOM], to_left),
        ][i]
        return pltpu.make_async_remote_copy(
            src_ref=source,
            dst_ref=target,
            send_sem=r_send.at[k, i],
            recv_sem=r_recv.at[k, i],
            device_id=to,
            device_id_type=MESH,
        )

    def start_sums(k):
        for i in range(4):
            sum_copy(k, i).start()

    def relay_sums(k):
        for i, to, shift in ((0, right, 0), (1, left, 8)):
            sum_copy(k, i).wait_recv()

            def body(j, carry, i=i, to=to, shift=shift):
                both = relay[k, i, j].astype(F32) + part[to, k, j + shift].astype(F32)
                relayed[k, i, j] = both.astype(BF16)
                return carry

            lax.fori_loop(0, 8, body, 0)
            sum_copy(k, 4 + i).start()

    def add_up(k):
        for i in range(2, 6):
            sum_copy(k, i).wait_recv()

        def body(i, carry):
            value = part[x, k, i].astype(F32) + out_bias[...]
            value = value + got[k, 0, i].astype(F32) + got[k, 1, i].astype(F32)
            summed[k, i] = value.astype(BF16)
            return carry

        lax.fori_loop(0, 16, body, 0)

    def start_owner(k):
        def body(j, carry):
            ps, pq = peer(j)
            pltpu.make_async_remote_copy(
                src_ref=summed.at[k, pq],
                dst_ref=rows.at[k, q * 2 + s],
                send_sem=v_send.at[k],
                recv_sem=v_recv.at[k],
                device_id={"section": ps, "seq": pq, "mp": x},
                device_id_type=MESH,
            ).start()
            return carry

        lax.fori_loop(1, 32, body, 0)
        pltpu.make_async_copy(summed.at[k, q], rows.at[k, q * 2 + s], own_sem.at[k]).start()

    def place_rows(k):
        pltpu.make_async_copy(summed.at[k, q], rows.at[k, q * 2 + s], own_sem.at[k]).wait()
        pltpu.make_async_copy(rows.at[k, pl.ds(0, 31)], rows.at[k, pl.ds(0, 31)], v_recv.at[k]).wait()
        visual = visual_mask[k * 32 : (k + 1) * 32, :] > 0.5
        for b in range(32):
            own_text = text[b // 8, k * 32 : (k + 1) * 32, (b % 8) * 256 : (b % 8 + 1) * 256]
            out[k, x, b] = jnp.where(visual, rows[k, b].astype(F32), own_text.astype(F32)).astype(BF16)

    def row_copy(k, piece, origin, to, slot):
        block = out.at[k, origin] if piece is None else out.at[k, origin, pl.ds(piece * 16, 16)]
        return pltpu.make_async_remote_copy(
            src_ref=block,
            dst_ref=block,
            send_sem=g_send.at[k, slot],
            recv_sem=g_recv.at[k, slot],
            device_id=to,
            device_id_type=MESH,
        )

    def start_rows(k):
        row_copy(k, None, x, to_right, 0).start()
        row_copy(k, None, x, to_left, 1).start()

    def relay_rows(k):
        row_copy(k, None, left, to_right, 0).wait_recv()
        row_copy(k, 0, left, to_right, 2).start()
        row_copy(k, None, right, to_left, 1).wait_recv()
        row_copy(k, 1, right, to_left, 3).start()

    def project(k):
        row_copy(k, 0, across, to_right, 2).wait_recv()
        row_copy(k, 1, across, to_left, 3).wait_recv()

        def square(b, carry):
            values = out[k, :, b].reshape(128, 256).astype(F32)
            return carry + values * values

        squares = lax.fori_loop(0, 32, square, jnp.zeros((128, 256), F32), unroll=2)
        mean = jnp.sum(squares, axis=-1, keepdims=True) * (1.0 / 8192.0)
        scale = jnp.broadcast_to(lax.rsqrt(mean + 1e-06), (128, 256))

        total[...] = jnp.broadcast_to(bias[...], total.shape)

        def depth(i, carry):
            for j in range(4):
                b = i * 4 + j
                values = out[k, :, b].reshape(128, 256).astype(F32)
                normed[:, j * 256 : (j + 1) * 256] = (values * scale * gain[b]).astype(BF16)
            span = pl.ds(pl.multiple_of(i * 1024, 1024), 1024)
            total[:, :512] += jnp.dot(normed[...], wq[span, :], preferred_element_type=F32)
            total[:, 512:] += jnp.dot(normed[...], wkv[span, :], preferred_element_type=F32)
            return carry

        lax.fori_loop(0, 8, depth, 0)
        for m in range(4):
            here = slice(m * 32, (m + 1) * 32)
            there = slice(m * 96 + k * 32, m * 96 + (k + 1) * 32)
            cosine, sine = cos_ref[there, :], sin_ref[there, :]

            def rotate(values):
                return (values * cosine + pltpu.roll(values, 64, 1) * sine).astype(BF16)

            for h in range(4):
                cols = slice(h * 128, (h + 1) * 128)
                q_out[there, cols] = rotate(total[here, cols])

            @pl.when(s == 0)
            def _():
                kv_out[there, :] = rotate(total[here, 512:])

            @pl.when(s == 1)
            def _():
                kv_out[there, :] = total[here, 512:].astype(BF16)

            for j in range(8):
                e_out[there, j * 256 : (j + 1) * 256] = out[k, m, x * 8 + j]

    start_sums(0)
    relay_sums(0)
    start_sums(1)
    add_up(0)
    start_owner(0)
    relay_sums(1)
    start_sums(2)
    add_up(1)
    start_owner(1)
    pltpu.make_async_copy(text_ref, text, load_sem.at[0]).wait()
    place_rows(0)
    start_rows(0)
    relay_sums(2)
    add_up(2)
    start_owner(2)
    place_rows(1)
    start_rows(1)
    relay_rows(0)
    place_rows(2)
    start_rows(2)
    relay_rows(1)
    pltpu.make_async_copy(wq_ref, wq, load_sem.at[1]).wait()
    pltpu.make_async_copy(wk_ref, wkv, load_sem.at[2]).wait()
    project(0)
    relay_rows(2)
    project(1)
    project(2)
    for k in range(3):
        for i in range(6):
            sum_copy(k, i).wait_send()
        pltpu.make_async_copy(rows.at[k, pl.ds(0, 31)], rows.at[k, pl.ds(0, 31)], v_send.at[k]).wait()
        row_copy(k, None, x, to_right, 0).wait_send()
        row_copy(k, None, x, to_left, 1).wait_send()
        row_copy(k, 0, left, to_right, 2).wait_send()
        row_copy(k, 1, right, to_left, 3).wait_send()


def spread(part, out_bias, visual_mask, gain, bias, cos, sin, text, wq, wk, wv):
    dma = pltpu.SemaphoreType.DMA
    return pl.pallas_call(
        spread_kernel,
        out_shape=[
            jax.ShapeDtypeStruct((384, 512), BF16),
            jax.ShapeDtypeStruct((384, 128), BF16),
            jax.ShapeDtypeStruct((384, 2048), BF16),
        ],
        in_specs=[VMEM] * 7 + [ANY] * 4,
        out_specs=[VMEM] * 3,
        scratch_shapes=[
            pltpu.VMEM((3, 2, 8, GROUP, 256), BF16),
            pltpu.VMEM((3, 2, 8, GROUP, 256), BF16),
            pltpu.VMEM((3, 2, 16, GROUP, 256), BF16),
            pltpu.VMEM((3, 16, GROUP, 256), BF16),
            pltpu.VMEM((3, 32, GROUP, 256), BF16),
            pltpu.VMEM((4, 96, 2048), BF16),
            pltpu.VMEM((3, 4, 32, GROUP, 256), BF16),
            pltpu.VMEM((128, 1024), BF16),
            pltpu.VMEM((8192, 512), BF16),
            pltpu.VMEM((8192, 128), BF16),
            pltpu.VMEM((128, 640), F32),
            dma((3, 6)),
            dma((3, 6)),
            dma((3,)),
            dma((3,)),
            dma((3,)),
            dma((3, 4)),
            dma((3, 4)),
            dma((3,)),
        ],
        compiler_params=pltpu.CompilerParams(
            collective_id=2, has_side_effects=True, vmem_limit_bytes=60 * MIB
        ),
        name="spread",
    )(part, out_bias, visual_mask, gain, bias, cos, sin, text, wq, wk, wv)


def attention_kernel(q_ref, shard, o_ref, kv_ref, scores, peak, norm, total, *sems):
    torus = Torus(shard, kv_ref, sems)
    greet(torus.peers())
    torus.start()
    torus.run(lambda s, q: None)
    own = lax.axis_index("seq")
    rows = q_ref.shape[0]
    factor = HEAD**-0.5 * math.log2(math.e)

    def stage(h):
        first, second = h < 4, h >= 1
        a, b = h % 2, (h + 1) % 2
        if first:
            query = q_ref[:, h * HEAD : (h + 1) * HEAD]
            peak[a] = jnp.full((rows, 128), -jnp.inf, F32)
        if second:
            top = jnp.broadcast_to(jnp.max(peak[b], axis=1, keepdims=True) * factor, (rows, 128))
            norm[...] = jnp.zeros((rows, 128), F32)
            total[...] = jnp.zeros((rows, HEAD), F32)

        def block(j, masked):
            pair = pl.ds(2 * j, 2)
            if first:
                keys = kv_ref[0, pair].reshape(2 * rows, HEAD)
                found = lax.dot_general(
                    query, keys, (((1,), (1,)), ((), ())), preferred_element_type=F32
                )
                if masked:
                    row = lax.broadcasted_iota(jnp.int32, found.shape, 0)
                    col = lax.broadcasted_iota(jnp.int32, found.shape, 1)
                    found = jnp.where(col - row <= (own - 2 * j) * rows, found, -jnp.inf)
                scores[a, j] = found
                tiles = [found[:, i * 128 : (i + 1) * 128] for i in range(6)]
                high = jnp.maximum(jnp.maximum(tiles[0], tiles[1]), jnp.maximum(tiles[2], tiles[3]))
                peak[a] = jnp.maximum(peak[a], jnp.maximum(high, jnp.maximum(tiles[4], tiles[5])))
            if second:
                tiles = [
                    jnp.exp2(scores[b, j, :, i * 128 : (i + 1) * 128] * factor - top) for i in range(6)
                ]
                norm[...] += ((tiles[0] + tiles[1]) + (tiles[2] + tiles[3])) + (tiles[4] + tiles[5])
                weights = jnp.concatenate([tile.astype(BF16) for tile in tiles], axis=1)
                values = kv_ref[1, pair].reshape(2 * rows, HEAD)
                total[...] += jnp.dot(weights, values, preferred_element_type=F32)

        def body(j, carry):
            block(j, False)
            return carry

        last = lax.div(own, 2)
        lax.fori_loop(0, last, body, 0)
        block(last, True)
        if second:
            cols = slice((h - 1) * HEAD, h * HEAD)
            o_ref[:, cols] = (total[...] / jnp.sum(norm[...], axis=1, keepdims=True)).astype(BF16)

    for h in range(5):
        stage(h)
    torus.finish()


def attention(queries, shard):
    rows = queries.shape[0]
    return pl.pallas_call(
        attention_kernel,
        out_shape=jax.ShapeDtypeStruct(queries.shape, BF16),
        in_specs=[VMEM, VMEM],
        out_specs=VMEM,
        scratch_shapes=[
            pltpu.VMEM((2, 16, rows, HEAD), BF16),
            pltpu.VMEM((2, 8, rows, 2 * rows), F32),
            pltpu.VMEM((2, rows, HEAD), F32),
            pltpu.VMEM((rows, HEAD), F32),
            pltpu.VMEM((rows, HEAD), F32),
        ]
        + torus_sems(),
        compiler_params=pltpu.CompilerParams(
            collective_id=1, has_side_effects=True, vmem_limit_bytes=60 * MIB
        ),
        name="attention",
    )(queries, shard)


def local(
    patches,
    norm_gain,
    norm_shift,
    merge_in_weight,
    merge_in_bias,
    merge_out_weight,
    merge_out_bias,
    text_embeds,
    rms_gain,
    query_weight,
    query_bias,
    key_weight,
    key_bias,
    value_weight,
    value_bias,
    patch_counts,
    image_offsets,
):
    section = lax.axis_index("section")
    seq = lax.axis_index("seq")
    col = lax.axis_index("mp")
    own_rows = text_embeds.shape[0]
    tokens = patch_counts // 4
    first = jnp.arange(6144 // GROUP, dtype=jnp.int32) * GROUP
    image_a = jnp.sum((image_offsets[None, :] <= first[:, None]).astype(jnp.int32), axis=1) - 1
    image_b = jnp.minimum(image_a + 1, 15)
    pick_a = image_a[:, None] == jnp.arange(16, dtype=jnp.int32)[None, :]
    pick_b = image_b[:, None] == jnp.arange(16, dtype=jnp.int32)[None, :]
    offset_a = jnp.sum(jnp.where(pick_a, image_offsets[None, :], 0), axis=1)
    offset_b = jnp.sum(jnp.where(pick_b, image_offsets[None, :], 0), axis=1)
    begin_b = jnp.where(image_a == 15, GROUP, jnp.minimum(offset_b - first, GROUP))
    start_a = jnp.minimum(image_a * 256 + first - offset_a, 4096)
    start_b = image_b * 256 - begin_b
    own_positions = seq * own_rows + jnp.arange(own_rows, dtype=jnp.int32)
    block_positions = seq * own_rows + col * 96 + jnp.arange(96, dtype=jnp.int32)
    relative = block_positions[:, None] - image_offsets[None, :]
    is_visual = jnp.any((relative >= 0) & (relative < tokens[None, :]), axis=1)
    visual_mask = jnp.broadcast_to(is_visual[:, None].astype(F32), (96, 256))
    half_dim = HEAD // 2
    inv_freq = jnp.exp(jnp.arange(half_dim, dtype=F32) * (-2.0 * math.log(1000000.0) / HEAD))
    angles = own_positions.astype(F32)[:, None] * inv_freq[None, :]
    cosine, sine = jnp.cos(angles), jnp.sin(angles)
    cos_table = jnp.concatenate([cosine, cosine], axis=1)
    sin_table = jnp.concatenate([-sine, sine], axis=1)

    halves = merge_out_weight.reshape(merge_out_weight.shape[0], 2, 256)
    w_own = lax.dynamic_index_in_dim(halves, section, 1, keepdims=False)
    w_other = lax.ppermute(
        lax.dynamic_index_in_dim(halves, 1 - section, 1, keepdims=False), "section", [(0, 1), (1, 0)]
    )
    hidden = merge_in(patches, norm_gain, norm_shift, merge_in_weight, merge_in_bias)
    part, text_rows = merge_out(hidden, w_own, w_other, text_embeds, start_a, start_b, begin_b)
    out_bias = lax.dynamic_slice_in_dim(merge_out_bias, section * 256, 256, 0).astype(F32)[None, :]
    key_value_bias = jnp.where(section == 0, key_bias, value_bias)
    bias = jnp.concatenate([query_bias, key_value_bias]).astype(F32)[None, :]
    gain = rms_gain.astype(F32).reshape(32, 1, 256)
    queries, shard, embeds = spread(
        part,
        out_bias,
        visual_mask,
        gain,
        bias,
        cos_table,
        sin_table,
        text_rows,
        query_weight,
        key_weight,
        value_weight,
    )
    return (embeds, attention(queries, shard))


def solution(mesh):
    placed = (
        P("seq", None),
        P(),
        P(),
        P(None, ("section", "mp")),
        P(("section", "mp")),
        P(("section", "mp"), "seq"),
        P("seq"),
        P("seq", "mp"),
        P(),
        P(None, ("section", "mp")),
        P(("section", "mp")),
        P(None, "mp"),
        P("mp"),
        P(None, "mp"),
        P("mp"),
        P(),
        P(),
    )
    return jax.shard_map(
        local,
        mesh=mesh,
        in_specs=placed,
        out_specs=(P("seq", "mp"), P("seq", ("section", "mp"))),
        check_vma=False,
    )
```

time: 790 us -> 204 us (0.26)
  waiting for transfers between devices: 256 us -> 0.01 us
  blocking collectives: 252 us -> 0 us
  Pallas kernels: 0 us -> 185 us
  other arithmetic: 111 us -> 4.45 us
  matrix products: 67.6 us -> 0 us
  local copies, waits for them, and re-layouts: 77.6 us -> 11.1 us
  between operations: 14 us -> 0.86 us
    psum x1 -> x0, blocking collectives: 252 us -> none  [local(): visual = lax.psum(routed, ('section', 'mp')).astype(jnp.bfloat16)]
    pallas_call x0 -> x4, Pallas kernels: none -> 185 us  [the longest x1 92.8 us: spread(): pl.pallas_call(spread_kernel, out_shape=[jax.ShapeDtypeStruct((384, 512),...]
    all_to_all x1 -> x0, waiting for transfers between devices: 136 us -> none  [local(): lax.all_to_all(partial_value, 'seq', split_axis=0, concat_axis=1, tiled=T...]
    all_gather x4 -> x0, waiting for transfers between devices: 120 us -> none  [the longest x1 66.8 us: local(): whole_rows = lax.all_gather(embeds, 'mp', axis=1, tiled=True)]
    sub x1, other arithmetic: 88.2 us -> 0.01 us  [local(): jnp.sum((image_offsets[None, :] <= first[:, None]).astype(jnp.int32), axi...]
    dot_general x7 -> x0, matrix products: 67.6 us -> none  [the longest x3 19.2 us: project(): jnp.dot(normed_seq, weight, preferred_element_type=jnp.float32)]
    gather x1 -> x0, local copies, waits for them, and re-layouts: 29.7 us -> none  [local(): jnp.take(gathered, slot_rows, axis=0)]
    broadcast_in_dim x2 -> x4, local copies, waits for them, and re-layouts: 17.1 us -> 2.5 us  [the longest x1 0.72 us: local(): visual_mask = jnp.broadcast_to(is_visual[:, None].astype(F32), (96, 256))]
  transfers between devices with their start and end apart: 5 -> 1, of which waited for: 4 -> 0; matrix products, arithmetic and copies ran while one was open for 20% -> 3% of each run, Pallas kernels for 0% -> 6%
where the time goes in v2:
time: 204 us
  Pallas kernels  185 us (91%)
  local copies, waits for them, and re-layouts  11.1 us (5%)
  other arithmetic  4.45 us (2%)
  starting transfers between devices  2.28 us (1%)
    pallas_call x1, Pallas kernels, spread(): pl.pallas_call(spread_kernel, out_shape=[jax.ShapeDtypeStruct((384, 512),...  92.8 us
    pallas_call x1, Pallas kernels, attention(): pl.pallas_call(attention_kernel, out_shape=jax.ShapeDtypeStruct(queries.s...  41.4 us
    pallas_call x1, Pallas kernels, merge_out(): pl.pallas_call(merge_out_kernel, in_specs=[smem, smem, smem, VMEM, ANY, A...  38.5 us
    pallas_call x1, Pallas kernels, merge_in(): pl.pallas_call(merge_in_kernel, grid=(cols // step,), in_specs=[pl.BlockS...  12.5 us
    unnamed x28, local copies, waits for them, and re-layouts  5.16 us
  transfers between devices with their start and end apart: 1, of which 0 were waited for; matrix products, arithmetic and copies ran while one was open for 3% of the time, Pallas kernels for 6%

profile of v2, /device:TPU:105, one launch (start us, length us, event | category | flops | bytes accessed | tf_op | source)
XLA Modules:
  0.0 203.8 jit_solution(11506390469788317313)
XLA Ops:
  0.6 2.0 reshape.72
  2.7 0.0 copy-start.11
  2.7 0.0 copy-start.3
  2.7 0.0 copy-start.7
  2.7 0.0 copy-start.6
  2.7 0.0 copy-start.4
  2.7 0.0 copy-start.5
  2.8 0.0 copy-start.2
  2.8 0.0 copy-start.8
  2.8 0.0 copy-start.9
  2.8 1.4 constant_dynamic-slice_fusion
  4.2 0.1 copy.27
  4.2 2.3 %collective-permute-start = (bf16[640,256]{1,0:T(8,128)(2,1)S(1)}, bf16[640,256]{1,0:T(8,128)(2,1)S(1)}, u32[]{:S(2)}, u32[]{:S(2)}) collective-permute-start(bf16[640,256]{1,0:T(8,128)(2,1)S(1)} %bitcast.11), channel_id=1, source_target_pairs={{0,64},{64,0},{1,65},{65,1},{2,66},{66,2},{3,67},{67,3},{4,68},{68... | collective-permute-start | bytes 983048 | tf_op jit(solution)/shard_map/ppermute | solution.py:714
  6.5 0.0 copy-done.11
  6.6 0.0 copy-done.3
  6.6 0.1 fusion.2
  6.7 0.1 convert_reduce_fusion
  6.8 0.0 copy-done.7
  6.8 0.0 copy-done.6
  6.8 0.6 reshape.77.b_ref
  7.4 0.0 copy-done.4
  7.4 0.6 reshape.75.gain_ref
  8.0 0.0 copy-done.5
  8.0 0.6 reshape.76.shift_ref
  8.6 0.0 copy-done.2
  8.6 0.6 reshape.79
  9.2 0.8 copy.28
  10.0 0.0 copy-done.8
  10.0 0.0 copy-done.9
  10.0 0.6 maximum_convert_fusion.bias
  10.6 0.1 select_reduce_fusion
  10.7 0.8 fusion
  11.4 0.9 pad_maximum_fusion
  12.4 0.0 copy-start.10
  12.4 12.5 %merge_in.1.x_ref = bf16[256,640]{1,0:T(8,128)(2,1)} custom-call(bf16[1024,1280]{1,0:T(8,128)(2,1)} %x_ref.1, f32[1,1280]{1,0:T(1,128)} %reshape.75.gain_ref, f32[1,1280]{1,0:T(1,128)} %reshape.76.shift_ref, bf16[5120,640]{1,0:T(8,128)(2,1)} %w_ref.1, f32[1,640]{1,0:T(1,128)} %reshape.77.b_ref), custom_call_target="tpu_custom_call" | custom-call | tf_op jit(solution)/shard_map/merge_in/pallas_call | solution.py:67
  24.9 0.0 copy-done.10
  24.9 0.6 dynamic-slice_convert_fusion
  25.5 0.6 compare_select_fusion
  26.1 0.0 collective-permute-done.w_other
  26.1 0.7 copy-done.1
  26.9 38.5 %merge_out.1 = (bf16[4,3,16,32,256]{4,3,2,1,0:T(8,128)(2,1)}, bf16[4,96,2048]{2,1,0:T(8,128)(2,1)}) custom-call(s32[192]{0:T(256)} %get-tuple-element.21.start_a, s32[192]{0:T(256)} %get-tuple-element.20.start_b, s32[192]{0:T(256)} %get-tuple-element.19.begin_b, bf16[256,640]{1,0:T(8,128)(2,1)} %merge_in.1.x_ref, bf16[640,256]{1,0:T(8,128)(2,1)} %bitcast.10, ...), custom_call_target="tpu_custom_call" | custom-call | tf_op jit(solution)/shard_map/merge_out/pallas_call | solution.py:303
  65.4 0.7 broadcast_in_dim.65.visual_mask
  66.1 92.8 %spread.1 = (bf16[384,512]{1,0:T(8,128)(2,1)}, bf16[384,128]{1,0:T(8,128)(2,1)}, bf16[384,2048]{1,0:T(8,128)(2,1)}) custom-call(bf16[4,3,16,32,256]{4,3,2,1,0:T(8,128)(2,1)} %get-tuple-element.7.part, f32[1,256]{1,0:T(1,128)} %bitcast.13, f32[96,256]{1,0:T(8,128)} %broadcast_in_dim.65.visual_mask, f32[32,1,256]{2,1,0:T(1,128)} %bitcast.12, ...), custom_call_target="tpu_custom_call" | custom-call | tf_op jit(solution)/shard_map/spread/pallas_call | solution.py:547
  158.9 41.4 %attention.1 = bf16[384,512]{1,0:T(8,128)(2,1)} custom-call(bf16[384,512]{1,0:T(8,128)(2,1)} %get-tuple-element.10.q_ref, bf16[384,128]{1,0:T(8,128)(2,1)} %get-tuple-element.11.shard), custom_call_target="tpu_custom_call" | custom-call | tf_op jit(solution)/shard_map/attention/pallas_call | solution.py:646
  200.3 0.0 copy-start
  200.3 2.8 %copy.31 = bf16[384,2048]{1,0:T(8,128)(2,1)} copy(bf16[384,2048]{1,0:T(8,128)(2,1)} %get-tuple-element.28) | data formatting | bytes 3145728
  203.0 0.0 copy-done
  203.1 0.7 copy.32
  (10 shorter events, 0.1 us)
Async XLA Ops:
  2.7 3.9 %copy-start.11 = (s32[16]{0:T(128)S(1)}, s32[16]{0:T(128)}, u32[]{:S(2)}) copy-start(s32[16]{0:T(128)} %param.32) | copy-start | bytes 196
  2.7 3.9 %copy-start.3 = (s32[16]{0:T(128)S(1)}, s32[16]{0:T(128)}, u32[]{:S(2)}) copy-start(s32[16]{0:T(128)} %param.33) | copy-start | bytes 196
  2.7 4.1 %copy-start.7 = (bf16[512]{0:T(512)(128)(2,1)S(1)}, bf16[512]{0:T(512)(128)(2,1)}, u32[]{:S(2)}) copy-start(bf16[512]{0:T(512)(128)(2,1)} %param.27) | copy-start | bytes 3076
  2.7 4.1 %copy-start.6 = (bf16[640]{0:T(1024)(128)(2,1)S(1)}, bf16[640]{0:T(1024)(128)(2,1)}, u32[]{:S(2)}) copy-start(bf16[640]{0:T(1024)(128)(2,1)} %param.21) | copy-start | bytes 3844
  2.7 4.7 %copy-start.4 = (bf16[1280]{0:T(1024)(128)(2,1)S(1)}, bf16[1280]{0:T(1024)(128)(2,1)}, u32[]{:S(2)}) copy-start(bf16[1280]{0:T(1024)(128)(2,1)} %param.18) | copy-start | bytes 7684
  2.7 5.3 %copy-start.5 = (bf16[1280]{0:T(1024)(128)(2,1)S(1)}, bf16[1280]{0:T(1024)(128)(2,1)}, u32[]{:S(2)}) copy-start(bf16[1280]{0:T(1024)(128)(2,1)} %param.19) | copy-start | bytes 7684
  2.8 5.8 %copy-start.2 = (bf16[8192]{0:T(1024)(128)(2,1)S(1)}, bf16[8192]{0:T(1024)(128)(2,1)}, u32[]{:S(2)}) copy-start(bf16[8192]{0:T(1024)(128)(2,1)} %param.25) | copy-start | bytes 49156
  2.8 7.2 %copy-start.8 = (bf16[128]{0:T(256)(128)(2,1)S(1)}, bf16[128]{0:T(256)(128)(2,1)}, u32[]{:S(2)}) copy-start(bf16[128]{0:T(256)(128)(2,1)} %param.29) | copy-start | bytes 772
  2.8 7.2 %copy-start.9 = (bf16[128]{0:T(256)(128)(2,1)S(1)}, bf16[128]{0:T(256)(128)(2,1)}, u32[]{:S(2)}) copy-start(bf16[128]{0:T(256)(128)(2,1)} %param.31) | copy-start | bytes 772
  4.2 21.9 %collective-permute-start = (bf16[640,256]{1,0:T(8,128)(2,1)S(1)}, bf16[640,256]{1,0:T(8,128)(2,1)S(1)}, u32[]{:S(2)}, u32[]{:S(2)}) collective-permute-start(bf16[640,256]{1,0:T(8,128)(2,1)S(1)} %bitcast.11), channel_id=1, source_target_pairs={{0,64},{64,0},{1,65},{65,1},{2,66},{66,2},{3,67},{67,3},{4,68},{68... | collective-permute-start | bytes 983048 | tf_op jit(solution)/shard_map/ppermute | solution.py:714
  12.4 12.5 %copy-start.10 = (bf16[512]{0:T(512)(128)(2,1)S(1)}, bf16[512]{0:T(512)(128)(2,1)}, u32[]{:S(2)}) copy-start(bf16[512]{0:T(512)(128)(2,1)} %param.23) | copy-start | bytes 3076
  26.1 0.7 copy-start.1
  200.3 2.8 %copy-start = (bf16[384,512]{1,0:T(8,128)(2,1)S(1)}, bf16[384,512]{1,0:T(8,128)(2,1)}, u32[]{:S(2)}) copy-start(bf16[384,512]{1,0:T(8,128)(2,1)} %attention.1) | copy-start | bytes 1179652

commit v3 on v2

v3 whole, which is shorter than its diff:
```python
import math

import jax
import jax.numpy as jnp
from jax import lax
from jax.experimental import pallas as pl
from jax.experimental.pallas import tpu as pltpu
from jax.sharding import PartitionSpec as P

HEAD = 128
MESH = pl.DeviceIdType.MESH
MIB = 1024 * 1024
ANY = pl.BlockSpec(memory_space=pl.ANY)
VMEM = pl.BlockSpec(memory_space=pltpu.VMEM)
BF16 = jnp.bfloat16
F32 = jnp.float32


def coords():
    s = lax.axis_index("section")
    q = lax.axis_index("seq")
    z = lax.div(q, 4)
    y = s * 2 + lax.rem(lax.div(q, 2), 2)
    return z, y, lax.rem(q, 2), lax.axis_index("mp")


def place(z, y, c):
    return lax.div(y, 2), z * 4 + lax.rem(y, 2) * 2 + c


def device(z, y, c, x):
    s, q = place(z, y, c)
    return {"section": s, "seq": q, "mp": x}


def torus_sems():
    dma = pltpu.SemaphoreType.DMA
    return [dma((4,)), dma((4,)), dma((4, 4)), dma((4, 4)), dma((4, 4)), dma((4, 4)), dma]


class Torus:
    def __init__(self, x_ref, out_ref, sems, base, count):
        self.x_ref, self.out_ref = x_ref.at[pl.ds(base, count)], out_ref
        self.base, self.count = base, count
        self.a_send, self.a_recv, self.b_send, self.b_recv, self.s_send, self.s_recv, self.own_sem = sems
        self.z, self.y, self.c, self.x = coords()
        self.half = count // 2
        self.started = []
        self.sibling = device(self.z, self.y, 1 - self.c, self.x)

    def where(self, da, db, core):
        zz = lax.rem(self.z + da * (1 - core) + db * core + 8, 4)
        yy = lax.rem(self.y + da * core + db * (1 - core) + 8, 4)
        return place(zz, yy, core)

    def target(self, da, db):
        s, q = self.where(da, db, self.c)
        return {"section": s, "seq": q, "mp": self.x}

    def peers(self):
        return [self.target(1, 0), self.target(-1, 0), self.target(0, 1), self.target(0, -1), self.sibling]

    def view(self, da, db, core, part):
        s, q = self.where(da, db, core)
        if part is None:
            return self.out_ref.at[s, q, pl.ds(self.base, self.count)]
        return self.out_ref.at[s, q, pl.ds(self.base + part * self.half, self.half)]

    def send(self, da, db, part, send_sem, recv_sem, to):
        block = self.view(da, db, self.c, part)
        copy = pltpu.make_async_remote_copy(
            src_ref=self.x_ref if da == 0 and db == 0 else block,
            dst_ref=block,
            send_sem=send_sem,
            recv_sem=recv_sem,
            device_id=to,
            device_id_type=MESH,
        )
        copy.start()
        self.started.append(copy)

    def arrived(self, da, db, core, part, send_sem, recv_sem):
        block = self.view(da, db, core, part)
        pltpu.make_async_remote_copy(
            src_ref=block,
            dst_ref=block,
            send_sem=send_sem,
            recv_sem=recv_sem,
            device_id=self.sibling,
            device_id_type=MESH,
        ).wait_recv()

    def along_b(self, a, da):
        self.send(da, 0, None, self.b_send.at[a, 0], self.b_recv.at[a, 0], self.target(0, 1))
        self.send(da, 0, None, self.b_send.at[a, 1], self.b_recv.at[a, 1], self.target(0, -1))
        self.send(da, 0, None, self.s_send.at[a, 0], self.s_recv.at[a, 0], self.sibling)

    def start(self):
        self.send(0, 0, None, self.a_send.at[0], self.a_recv.at[0], self.target(1, 0))
        self.send(0, 0, None, self.a_send.at[1], self.a_recv.at[1], self.target(-1, 0))
        self.along_b(0, 0)
        self.own_copy = pltpu.make_async_copy(self.x_ref, self.view(0, 0, self.c, None), self.own_sem)
        self.own_copy.start()

    def run(self, use):
        offsets = [0, -1, 1, 2]
        c = self.c

        def from_sibling(a, b):
            da, db = offsets[a], offsets[b]
            self.arrived(da, db, 1 - c, None, self.s_send.at[a, b], self.s_recv.at[a, b])
            use(*self.where(da, db, 1 - c))

        def relay_b(a):
            da = offsets[a]
            self.arrived(da, -1, c, None, self.b_send.at[a, 0], self.b_recv.at[a, 0])
            self.send(da, -1, 0, self.b_send.at[a, 2], self.b_recv.at[a, 2], self.target(0, 1))
            self.send(da, -1, None, self.s_send.at[a, 1], self.s_recv.at[a, 1], self.sibling)
            self.arrived(da, 1, c, None, self.b_send.at[a, 1], self.b_recv.at[a, 1])
            self.send(da, 1, 1, self.b_send.at[a, 3], self.b_recv.at[a, 3], self.target(0, -1))
            self.send(da, 1, None, self.s_send.at[a, 2], self.s_recv.at[a, 2], self.sibling)
            use(*self.where(da, -1, c))
            use(*self.where(da, 1, c))

        self.own_copy.wait()
        use(*self.where(0, 0, c))
        self.arrived(-1, 0, c, None, self.a_send.at[0], self.a_recv.at[0])
        self.send(-1, 0, 0, self.a_send.at[2], self.a_recv.at[2], self.target(1, 0))
        self.along_b(1, -1)
        self.arrived(1, 0, c, None, self.a_send.at[1], self.a_recv.at[1])
        self.send(1, 0, 1, self.a_send.at[3], self.a_recv.at[3], self.target(-1, 0))
        self.along_b(2, 1)
        use(*self.where(-1, 0, c))
        use(*self.where(1, 0, c))
        from_sibling(0, 0)
        yield
        relay_b(0)
        yield
        self.arrived(2, 0, c, 0, self.a_send.at[2], self.a_recv.at[2])
        self.arrived(2, 0, c, 1, self.a_send.at[3], self.a_recv.at[3])
        self.along_b(3, 2)
        use(*self.where(2, 0, c))
        from_sibling(1, 0)
        from_sibling(2, 0)
        for a in (1, 2, 3):
            relay_b(a)
            from_sibling(a - 1, 1)
            from_sibling(a - 1, 2)
            yield
        from_sibling(3, 0)
        from_sibling(3, 1)
        from_sibling(3, 2)
        for a in range(4):
            da = offsets[a]
            self.arrived(da, 2, c, 0, self.b_send.at[a, 2], self.b_recv.at[a, 2])
            self.arrived(da, 2, c, 1, self.b_send.at[a, 3], self.b_recv.at[a, 3])
            self.send(da, 2, None, self.s_send.at[a, 3], self.s_recv.at[a, 3], self.sibling)
            use(*self.where(da, 2, c))
        for a in range(4):
            from_sibling(a, 3)

    def finish(self):
        for copy in self.started:
            copy.wait_send()


def greet(peers):
    barrier = pltpu.get_barrier_semaphore()
    for peer in peers:
        pl.semaphore_signal(barrier, inc=1, device_id=peer, device_id_type=MESH)
    pl.semaphore_wait(barrier, len(peers))


class CrossSum:
    def __init__(self, staged, relay, relayed, got, sums, bias, send_sem, recv_sem):
        self.staged, self.relay, self.relayed, self.got, self.sums = staged, relay, relayed, got, sums
        self.bias, self.send_sem, self.recv_sem = bias, send_sem, recv_sem
        z, y, c, x = coords()
        self.x = x
        self.right, self.left, self.across = lax.rem(x + 1, 4), lax.rem(x + 3, 4), lax.rem(x + 2, 4)
        self.to_right, self.to_left = device(z, y, c, self.right), device(z, y, c, self.left)

    def copy(self, g, i):
        top, bottom = pl.ds(0, 128), pl.ds(128, 128)
        staged, got, sums = self.staged.at[g], self.got.at[g], self.sums.at[g]
        source, target, to = [
            (staged.at[self.across, top], self.relay.at[g, 0], self.to_right),
            (staged.at[self.across, bottom], self.relay.at[g, 1], self.to_left),
            (staged.at[self.right, bottom], got.at[0, bottom], self.to_right),
            (staged.at[self.left, top], got.at[1, top], self.to_left),
            (self.relayed.at[g, 0], got.at[0, top], self.to_right),
            (self.relayed.at[g, 1], got.at[1, bottom], self.to_left),
            (sums.at[self.x], sums.at[self.x], self.to_right),
            (sums.at[self.x], sums.at[self.x], self.to_left),
            (sums.at[self.left, top], sums.at[self.left, top], self.to_right),
            (sums.at[self.right, bottom], sums.at[self.right, bottom], self.to_left),
        ][i]
        return pltpu.make_async_remote_copy(
            src_ref=source,
            dst_ref=target,
            send_sem=self.send_sem.at[g, i],
            recv_sem=self.recv_sem.at[g, i],
            device_id=to,
            device_id_type=MESH,
        )

    def landed(self, g, origin, part, i):
        block = self.sums.at[g, origin] if part is None else self.sums.at[g, origin, pl.ds(part * 128, 128)]
        pltpu.make_async_remote_copy(
            src_ref=block,
            dst_ref=block,
            send_sem=self.send_sem.at[g, i],
            recv_sem=self.recv_sem.at[g, i],
            device_id=self.to_right,
            device_id_type=MESH,
        ).wait_recv()

    def start(self, g):
        for i in range(4):
            self.copy(g, i).start()

    def pass_on(self, g):
        for i, to in ((0, self.right), (1, self.left)):
            self.copy(g, i).wait_recv()

            def body(j, carry, i=i, to=to):
                here = pl.ds(pl.multiple_of(j * 32, 32), 32)
                there = pl.ds(pl.multiple_of(j * 32 + i * 128, 32), 32)
                both = self.relay[g, i, here, :].astype(F32) + self.staged[g, to, there, :].astype(F32)
                self.relayed[g, i, here, :] = both.astype(BF16)
                return carry

            lax.fori_loop(0, 4, body, 0)
            self.copy(g, 4 + i).start()

    def add_up(self, g):
        for i in range(2, 6):
            self.copy(g, i).wait_recv()

        def body(j, carry):
            here = pl.ds(pl.multiple_of(j * 32, 32), 32)
            value = self.staged[g, self.x, here, :].astype(F32) + self.bias
            value = value + self.got[g, 0, here, :].astype(F32) + self.got[g, 1, here, :].astype(F32)
            self.sums[g, self.x, here, :] = value.astype(BF16)
            return carry

        lax.fori_loop(0, 8, body, 0)
        self.copy(g, 6).start()
        self.copy(g, 7).start()

    def spread(self, g):
        self.landed(g, self.left, None, 6)
        self.copy(g, 8).start()
        self.landed(g, self.right, None, 7)
        self.copy(g, 9).start()

    def done(self, g):
        self.landed(g, self.across, 0, 8)
        self.landed(g, self.across, 1, 9)

    def finish(self, g):
        for i in range(10):
            self.copy(g, i).wait_send()


GROUP = 32


def merger_kernel(
    offsets, vecs, patches_ref, w_in_ref, w_out_ref, text,
    part, text_rows, text_last,
    x_buf, w_in, normed, joined, shard, hidden, weight, product, staged, relay, relayed, got, sums,
    t_send, t_recv, w_sem, c_send, c_recv, *sems
):
    halves = [Torus(shard, hidden, sems[h * 7 : h * 7 + 7], h * 128, 128) for h in range(2)]
    z, y, c, x = coords()
    section = lax.div(y, 2)
    cross = CrossSum(
        staged, relay, relayed, got, sums,
        vecs[:, pl.ds(pl.multiple_of(3200 + section * 256, 128), 256)], c_send, c_recv,
    )
    load_x = [
        pltpu.make_async_copy(patches_ref.at[pl.ds(h * 512, 512)], x_buf.at[pl.ds(h * 512, 512)], w_sem.at[5 + h])
        for h in range(2)
    ]
    load_w = [
        pltpu.make_async_copy(w_in_ref.at[pl.ds(i * 1280, 1280)], w_in.at[pl.ds(i * 1280, 1280)], w_sem.at[7 + i])
        for i in range(4)
    ]
    for load in load_x + load_w:
        load.start()
    other = device(z, lax.rem(y + 2, 4), c, x)
    greet(halves[0].peers() + [device(z, y, c, lax.rem(x + d, 4)) for d in (1, 2, 3)] + [other])

    def half_of(s):
        return w_out_ref.at[:, pl.ds(pl.multiple_of(s * 256, 256), 256)]

    swap = pltpu.make_async_remote_copy(
        src_ref=half_of(1 - section),
        dst_ref=weight.at[1],
        send_sem=w_sem.at[2],
        recv_sem=w_sem.at[3],
        device_id=other,
        device_id_type=MESH,
    )
    swap.start()
    keep = pltpu.make_async_copy(half_of(section), weight.at[0], w_sem.at[4])
    keep.start()

    def text_copy(d, last):
        to = lax.rem(x + d, 4)
        if last:
            source, target = text.at[pl.ds(256, 128)], text_last.at[x]
        else:
            source, target = text.at[pl.ds(pl.multiple_of(to * 64, 64), 64)], text_rows.at[x]
        return pltpu.make_async_remote_copy(
            src_ref=source,
            dst_ref=target,
            send_sem=t_send.at[last, d],
            recv_sem=t_recv.at[last, d],
            device_id=device(z, y, c, to),
            device_id_type=MESH,
        )

    for last in (0, 1):
        for d in (1, 2, 3):
            text_copy(d, last).start()

    width = patches_ref.shape[1]
    tiles = width // 128
    gain, shift = vecs[:, :1280], vecs[:, 1280:2560]
    def norm(h, first, last):
        def body(i, carry):
            from_row = pl.ds(pl.multiple_of(h * 512 + i * 64, 64), 64)
            to_row = pl.ds(pl.multiple_of(i * 64, 64), 64)
            values = x_buf[from_row, :].astype(F32)
            center = values - jnp.mean(values, axis=-1, keepdims=True)
            spread = jnp.mean(center * center, axis=-1, keepdims=True)
            result = center * lax.rsqrt(spread + 1e-06) * gain + shift
            for u in range(tiles):
                normed[u, to_row, :] = result[:, u * 128 : (u + 1) * 128]
            return carry

        lax.fori_loop(first, last, body, 0)

    def join():
        for t in range(4):
            for u in range(tiles):
                cols = slice((t * tiles + u) * 128, (t * tiles + u + 1) * 128)
                joined[:, cols] = normed[u, pl.ds(t, 128, stride=4), :].astype(BF16)

    def multiply(h, first):
        cols = slice(first, min(first + 256, 640))
        total = jnp.dot(joined[...], w_in[:, cols], preferred_element_type=F32)
        total = total + vecs[:, 2560 + cols.start : 2560 + cols.stop]
        shard[h * 128 : (h + 1) * 128, cols] = (0.5 * total * (1.0 + lax.erf(total * (2.0**-0.5)))).astype(BF16)

    def use(h):
        def multiply_out(s, q):
            block = hidden[s, q, h * 128 : (h + 1) * 128, :]
            total = jnp.dot(block, weight[lax.rem(s + section, 2)], preferred_element_type=F32)
            rows = pl.ds(pl.multiple_of(q * 256 + h * 128, 128), 128)
            for half in range(2):
                product[half, rows, :] += total[:, half * 128 : (half + 1) * 128]

        return multiply_out

    runs = [halves[h].run(use(h)) for h in range(2)]
    load_x[0].wait()
    norm(0, 0, 8)
    join()
    for load in load_w:
        load.wait()
    for first in (0, 256, 512):
        multiply(0, first)
    halves[0].start()
    product[...] = jnp.zeros(product.shape, F32)
    load_x[1].wait()
    norm(1, 0, 8)
    keep.wait()
    swap.wait()
    next(runs[0])
    join()
    multiply(1, 0)
    next(runs[0])
    multiply(1, 256)
    multiply(1, 512)
    next(runs[0])
    next(runs[0])
    halves[1].start()
    for _ in runs[0]:
        pass

    def rows_of(g, n, m):
        return pl.ds((g % 2 * 8 + n) * 256 + g // 2 * 128 + m * 32, 32)

    def stage(g):
        for n in range(8):
            for m in range(4):
                for half in range(2):
                    cols = slice(half * 128, (half + 1) * 128)
                    staged[g, m, n * 32 : (n + 1) * 32, cols] = product[half, rows_of(g, n, m), :].astype(BF16)
        cross.start(g)

    def unstage(g):
        cross.done(g)
        for n in range(8):
            for m in range(4):
                for half in range(2):
                    cols = slice(half * 128, (half + 1) * 128)
                    product[half, rows_of(g, n, m), :] = sums[g, m, n * 32 : (n + 1) * 32, cols].astype(F32)

    stage(0)
    stage(1)
    next(runs[1])
    next(runs[1])
    cross.pass_on(0)
    cross.pass_on(1)
    next(runs[1])
    next(runs[1])
    cross.add_up(0)
    cross.add_up(1)
    next(runs[1])
    cross.spread(0)
    cross.spread(1)
    for _ in runs[1]:
        pass
    stage(2)
    stage(3)
    unstage(0)
    unstage(1)
    cross.pass_on(2)
    cross.pass_on(3)
    cross.add_up(2)
    cross.add_up(3)
    cross.spread(2)
    cross.spread(3)
    unstage(2)
    unstage(3)
    row = lax.broadcasted_iota(jnp.int32, (GROUP, 128), 0)

    def body(q, image_a):
        for i in range(12):
            k, m = (i % 2, i // 2) if i < 8 else (2, i - 8)
            first = q * 384 + i * GROUP
            following = jnp.minimum(image_a + 1, 15)
            image_a = jnp.where(offsets[following] <= first, following, image_a)
            image_b = jnp.minimum(image_a + 1, 15)
            begin = jnp.where(image_a == 15, GROUP, jnp.clip(offsets[image_b] - first, 0, GROUP))
            start_a = jnp.clip(image_a * 256 + first - offsets[image_a], 0, 4096)
            start_b = jnp.clip(image_b * 256 - begin, 0, 4096)
            for half in range(2):
                one = product[half, pl.ds(start_a, GROUP), :]
                two = product[half, pl.ds(start_b, GROUP), :]
                cols = slice(half * 128, (half + 1) * 128)
                part[k, q, m, :, cols] = jnp.where(row >= begin, two, one).astype(BF16)
        return image_a

    lax.fori_loop(0, 16, body, jnp.int32(0))
    for torus in halves:
        torus.finish()
    for g in range(4):
        cross.finish(g)
    for last, target in ((0, text_rows), (1, text_last)):
        for d in (1, 2, 3):
            block = target.at[lax.rem(x + 4 - d, 4)]
            pltpu.make_async_remote_copy(
                src_ref=block,
                dst_ref=block,
                send_sem=t_send.at[last, d],
                recv_sem=t_recv.at[last, d],
                device_id=other,
                device_id_type=MESH,
            ).wait_recv()
            text_copy(d, last).wait_send()


def merger(offsets, vecs, patches, w_in, w_out, text):
    dma = pltpu.SemaphoreType.DMA
    return pl.pallas_call(
        merger_kernel,
        in_specs=[pl.BlockSpec(memory_space=pltpu.SMEM), VMEM, ANY, ANY, ANY, ANY],
        out_specs=[VMEM, ANY, ANY],
        out_shape=[
            jax.ShapeDtypeStruct((3, 16, 4, GROUP, 256), BF16),
            jax.ShapeDtypeStruct((4, 64, 2048), BF16),
            jax.ShapeDtypeStruct((4, 128, 2048), BF16),
        ],
        scratch_shapes=[
            pltpu.VMEM((1024, 1280), BF16),
            pltpu.VMEM((5120, 640), BF16),
            pltpu.VMEM((10, 512, 128), F32),
            pltpu.VMEM((128, 5120), BF16),
            pltpu.VMEM((256, 640), BF16),
            pltpu.VMEM((2, 16, 256, 640), BF16),
            pltpu.VMEM((2, 640, 256), BF16),
            pltpu.VMEM((2, 4096 + GROUP, 128), F32),
            pltpu.VMEM((4, 4, 256, 256), BF16),
            pltpu.VMEM((4, 2, 128, 256), BF16),
            pltpu.VMEM((4, 2, 128, 256), BF16),
            pltpu.VMEM((4, 2, 256, 256), BF16),
            pltpu.VMEM((4, 4, 256, 256), BF16),
            dma((2, 4)),
            dma((2, 4)),
            dma((11,)),
            dma((4, 10)),
            dma((4, 10)),
        ]
        + torus_sems()
        + torus_sems(),
        compiler_params=pltpu.CompilerParams(
            collective_id=0, has_side_effects=True, vmem_limit_bytes=60 * MIB
        ),
        name="merger",
    )(offsets, vecs, patches, w_in, w_out, text)


def spread_kernel(
    offsets, counts, vecs, cos_ref, sin_ref, part, text_ref, text_last_ref, own_text, wq_ref, wk_ref, wv_ref,
    q_out, kv_out, e_hbm,
    e_out, rows, rows_last, text, text_last, out, normed, wq, wkv, total,
    v_send, v_recv, own_sem, g_send, g_recv, load_sem, text_sem,
):
    z, y, c, x = coords()
    s, q = place(z, y, c)
    linear = s * 16 + q
    right, left, across = lax.rem(x + 1, 4), lax.rem(x + 3, 4), lax.rem(x + 2, 4)
    to_right, to_left = device(z, y, c, right), device(z, y, c, left)
    load_text, load_last = [], []
    for d in range(4):
        slot = lax.rem(x + d, 4)
        near, last = text_ref.at[slot], text_last_ref.at[slot]
        if d == 0:
            near = own_text.at[pl.ds(pl.multiple_of(x * 64, 64), 64)]
            last = own_text.at[pl.ds(256, 128)]
        load_text.append(pltpu.make_async_copy(near, text.at[slot], text_sem.at[0, d]))
        load_last.append(pltpu.make_async_copy(last, text_last.at[slot], text_sem.at[1, d]))
    load_q = pltpu.make_async_copy(wq_ref, wq, load_sem.at[1])
    for load in load_text + load_last + [load_q]:
        load.start()

    @pl.when(s == 0)
    def _():
        pltpu.make_async_copy(wk_ref, wkv, load_sem.at[2]).start()

    @pl.when(s == 1)
    def _():
        pltpu.make_async_copy(wv_ref, wkv, load_sem.at[2]).start()

    def peer(j):
        other = lax.rem(linear + j, 32)
        return lax.div(other, 16), lax.rem(other, 16)

    barrier = pltpu.get_barrier_semaphore()
    for to in (to_right, to_left):
        pl.semaphore_signal(barrier, inc=1, device_id=to, device_id_type=MESH)

    def hello(j, carry):
        ps, pq = peer(j)
        pl.semaphore_signal(
            barrier, inc=1, device_id={"section": ps, "seq": pq, "mp": x}, device_id_type=MESH
        )
        return carry

    lax.fori_loop(1, 32, hello, 0)
    pl.semaphore_wait(barrier, 33)

    def own_copy(k):
        if k < 2:
            return pltpu.make_async_copy(part.at[k, q, x], rows.at[k, q * 2 + s], own_sem.at[k])
        return pltpu.make_async_copy(part.at[k, q], rows_last.at[q * 2 + s], own_sem.at[k])

    def start_owner(k):
        def body(j, carry):
            ps, pq = peer(j)
            pltpu.make_async_remote_copy(
                src_ref=part.at[k, pq, x] if k < 2 else part.at[k, pq],
                dst_ref=rows.at[k, q * 2 + s] if k < 2 else rows_last.at[q * 2 + s],
                send_sem=v_send.at[k],
                recv_sem=v_recv.at[k],
                device_id={"section": ps, "seq": pq, "mp": x},
                device_id_type=MESH,
            ).start()
            return carry

        lax.fori_loop(1, 32, body, 0)
        own_copy(k).start()

    def visual_rows(first):
        position = q * 384 + first + lax.broadcasted_iota(jnp.int32, (GROUP, 256), 0)
        found = jnp.zeros((GROUP, 256), jnp.int32)
        for i in range(16):
            begin = offsets[i]
            inside = (position >= begin) & (position < begin + lax.div(counts[i], 4))
            found = jnp.where(inside, 1, found)
        return found > 0

    def others(k):
        return rows.at[k, pl.ds(0, 31)] if k < 2 else rows_last.at[pl.ds(0, 31)]

    def place_rows(k):
        own_copy(k).wait()
        pltpu.make_async_copy(others(k), others(k), v_recv.at[k]).wait()
        if k < 2:
            visual = visual_rows(x * 64 + k * 32)
            for b in range(32):
                own_text = text[b // 8, k * 32 : (k + 1) * 32, (b % 8) * 256 : (b % 8 + 1) * 256]
                out[k, x, b] = jnp.where(visual, rows[k, b].astype(F32), own_text.astype(F32)).astype(BF16)
        else:
            for m in range(4):
                visual = visual_rows(256 + m * 32)
                for b in range(32):
                    own_text = text_last[b // 8, m * 32 : (m + 1) * 32, (b % 8) * 256 : (b % 8 + 1) * 256]
                    picked = jnp.where(visual, rows_last[b, m].astype(F32), own_text.astype(F32))
                    out[k, m, b] = picked.astype(BF16)

    def row_copy(k, piece, origin, to, slot):
        block = out.at[k, origin] if piece is None else out.at[k, origin, pl.ds(piece * 16, 16)]
        return pltpu.make_async_remote_copy(
            src_ref=block,
            dst_ref=block,
            send_sem=g_send.at[k, slot],
            recv_sem=g_recv.at[k, slot],
            device_id=to,
            device_id_type=MESH,
        )

    def start_rows(k):
        row_copy(k, None, x, to_right, 0).start()
        row_copy(k, None, x, to_left, 1).start()

    def relay_rows(k):
        row_copy(k, None, left, to_right, 0).wait_recv()
        row_copy(k, 0, left, to_right, 2).start()
        row_copy(k, None, right, to_left, 1).wait_recv()
        row_copy(k, 1, right, to_left, 3).start()

    def project(k):
        if k < 2:
            row_copy(k, 0, across, to_right, 2).wait_recv()
            row_copy(k, 1, across, to_left, 3).wait_recv()

        def square(b, carry):
            values = out[k, :, b].reshape(128, 256).astype(F32)
            return carry + values * values

        squares = lax.fori_loop(0, 32, square, jnp.zeros((128, 256), F32), unroll=2)
        mean = jnp.sum(squares, axis=-1, keepdims=True) * (1.0 / 8192.0)
        scale = jnp.broadcast_to(lax.rsqrt(mean + 1e-06), (128, 256))

        total[...] = jnp.broadcast_to(vecs[:, 3712:4352], total.shape)

        def depth(i, carry):
            for j in range(4):
                b = i * 4 + j
                values = out[k, :, b].reshape(128, 256).astype(F32)
                gain = vecs[:, pl.ds(pl.multiple_of(4352 + b * 256, 128), 256)]
                normed[:, j * 256 : (j + 1) * 256] = (values * scale * gain).astype(BF16)
            span = pl.ds(pl.multiple_of(i * 1024, 1024), 1024)
            total[:, :512] += jnp.dot(normed[...], wq[span, :], preferred_element_type=F32)
            total[:, 512:] += jnp.dot(normed[...], wkv[span, :], preferred_element_type=F32)
            return carry

        lax.fori_loop(0, 8, depth, 0)
        for m in range(4):
            here = slice(m * 32, (m + 1) * 32)
            there = pl.ds(m * 64 + k * 32 if k < 2 else 256 + m * 32, 32)
            cosine, sine = cos_ref[there, :], sin_ref[there, :]

            def rotate(values):
                return (values * cosine + pltpu.roll(values, 64, 1) * sine).astype(BF16)

            for h in range(4):
                cols = slice(h * 128, (h + 1) * 128)
                q_out[there, cols] = rotate(total[here, cols])

            @pl.when(s == 0)
            def _():
                kv_out[there, :] = rotate(total[here, 512:])

            @pl.when(s == 1)
            def _():
                kv_out[there, :] = total[here, 512:].astype(BF16)

            for j in range(8):
                e_out[there, j * 256 : (j + 1) * 256] = out[k, m, x * 8 + j]

    for k in range(3):
        start_owner(k)
    for load in load_text:
        load.wait()
    place_rows(0)
    start_rows(0)
    place_rows(1)
    start_rows(1)
    relay_rows(0)
    for load in load_last:
        load.wait()
    place_rows(2)
    relay_rows(1)
    load_q.wait()
    pltpu.make_async_copy(wk_ref, wkv, load_sem.at[2]).wait()
    project(2)
    project(0)
    project(1)
    save = pltpu.make_async_copy(e_out, e_hbm, load_sem.at[4])
    save.start()
    for k in range(3):
        pltpu.make_async_copy(others(k), others(k), v_send.at[k]).wait()
    for k in range(2):
        row_copy(k, None, x, to_right, 0).wait_send()
        row_copy(k, None, x, to_left, 1).wait_send()
        row_copy(k, 0, left, to_right, 2).wait_send()
        row_copy(k, 1, right, to_left, 3).wait_send()
    save.wait()


def spread(offsets, counts, vecs, cos, sin, part, text, text_last, own_text, wq, wk, wv):
    dma = pltpu.SemaphoreType.DMA
    smem = pl.BlockSpec(memory_space=pltpu.SMEM)
    return pl.pallas_call(
        spread_kernel,
        out_shape=[
            jax.ShapeDtypeStruct((384, 512), BF16),
            jax.ShapeDtypeStruct((384, 128), BF16),
            jax.ShapeDtypeStruct((384, 2048), BF16),
        ],
        in_specs=[smem, smem, VMEM, VMEM, VMEM, VMEM] + [ANY] * 6,
        out_specs=[VMEM, VMEM, ANY],
        scratch_shapes=[
            pltpu.VMEM((384, 2048), BF16),
            pltpu.VMEM((2, 32, GROUP, 256), BF16),
            pltpu.VMEM((32, 4, GROUP, 256), BF16),
            pltpu.VMEM((4, 64, 2048), BF16),
            pltpu.VMEM((4, 128, 2048), BF16),
            pltpu.VMEM((3, 4, 32, GROUP, 256), BF16),
            pltpu.VMEM((128, 1024), BF16),
            pltpu.VMEM((8192, 512), BF16),
            pltpu.VMEM((8192, 128), BF16),
            pltpu.VMEM((128, 640), F32),
            dma((3,)),
            dma((3,)),
            dma((3,)),
            dma((2, 4)),
            dma((2, 4)),
            dma((5,)),
            dma((2, 4)),
        ],
        compiler_params=pltpu.CompilerParams(
            collective_id=2, has_side_effects=True, vmem_limit_bytes=60 * MIB
        ),
        name="spread",
    )(offsets, counts, vecs, cos, sin, part, text, text_last, own_text, wq, wk, wv)


def attention_kernel(q_ref, shard, o_ref, kv_ref, scores, peak, *sems):
    torus = Torus(shard, kv_ref, sems, 0, shard.shape[0])
    greet(torus.peers())
    torus.start()
    own = lax.axis_index("seq")
    rows = q_ref.shape[0]
    factor = HEAD**-0.5 * math.log2(math.e)
    peak[...] = jnp.full(peak.shape, -jnp.inf, F32)

    def score(j, masked):
        for h in range(4):
            query = q_ref[:, h * HEAD : (h + 1) * HEAD]
            found = lax.dot_general(
                query, kv_ref[0, j], (((1,), (1,)), ((), ())), preferred_element_type=F32
            )
            if masked:
                row = lax.broadcasted_iota(jnp.int32, found.shape, 0)
                col = lax.broadcasted_iota(jnp.int32, found.shape, 1)
                found = jnp.where(col <= row, found, -jnp.inf)
            scores[h, j] = found
            tiles = [found[:, i * 128 : (i + 1) * 128] for i in range(3)]
            peak[h] = jnp.maximum(jnp.maximum(peak[h], tiles[0]), jnp.maximum(tiles[1], tiles[2]))

    def use(s, q):
        @pl.when((s == 0) & (q < own))
        def _():
            score(q, False)

    for _ in torus.run(use):
        pass
    score(own, True)
    after = own + 1

    @pl.when(lax.rem(own, 2) == 0)
    def _():
        for h in range(4):
            scores[h, after] = jnp.full((rows, rows), -jnp.inf, F32)

    for h in range(4):
        top = jnp.broadcast_to(jnp.max(peak[h], axis=1, keepdims=True) * factor, (rows, 128))

        def pair(j, carry):
            norm, total = carry
            tiles = [
                jnp.exp2(scores[h, 2 * j + i // 3, :, i % 3 * 128 : (i % 3 + 1) * 128] * factor - top)
                for i in range(6)
            ]
            norm = norm + (((tiles[0] + tiles[1]) + (tiles[2] + tiles[3])) + (tiles[4] + tiles[5]))
            weights = jnp.concatenate([tile.astype(BF16) for tile in tiles], axis=1)
            values = kv_ref[1, pl.ds(2 * j, 2)].reshape(2 * rows, HEAD)
            return norm, total + jnp.dot(weights, values, preferred_element_type=F32)

        start = (jnp.zeros((rows, 128), F32), jnp.zeros((rows, HEAD), F32))
        norm, total = lax.fori_loop(0, lax.div(own, 2) + 1, pair, start)
        cols = slice(h * HEAD, (h + 1) * HEAD)
        o_ref[:, cols] = (total / jnp.sum(norm, axis=1, keepdims=True)).astype(BF16)
    torus.finish()


def attention(queries, shard):
    rows = queries.shape[0]
    return pl.pallas_call(
        attention_kernel,
        out_shape=jax.ShapeDtypeStruct(queries.shape, BF16),
        in_specs=[VMEM, VMEM],
        out_specs=VMEM,
        scratch_shapes=[
            pltpu.VMEM((2, 16, rows, HEAD), BF16),
            pltpu.VMEM((4, 16, rows, rows), F32),
            pltpu.VMEM((4, rows, HEAD), F32),
        ]
        + torus_sems(),
        compiler_params=pltpu.CompilerParams(
            collective_id=1, has_side_effects=True, vmem_limit_bytes=60 * MIB
        ),
        name="attention",
    )(queries, shard)


def local(
    patches,
    norm_gain,
    norm_shift,
    merge_in_weight,
    merge_in_bias,
    merge_out_weight,
    merge_out_bias,
    text_embeds,
    rms_gain,
    query_weight,
    query_bias,
    key_weight,
    key_bias,
    value_weight,
    value_bias,
    patch_counts,
    image_offsets,
):
    section = lax.axis_index("section")
    own_rows = text_embeds.shape[0]
    positions = lax.axis_index("seq") * own_rows + jnp.arange(own_rows, dtype=jnp.int32)
    column = jnp.arange(HEAD, dtype=jnp.int32)
    inv_freq = jnp.exp((column % 64).astype(F32) * (-2.0 * math.log(1000000.0) / HEAD))
    angles = positions.astype(F32)[:, None] * inv_freq[None, :]
    cosine = jnp.cos(angles)
    sine = jnp.where(column < 64, -1.0, 1.0)[None, :] * jnp.sin(angles)
    key_value_bias = jnp.where(section == 0, key_bias, value_bias)
    pieces = [norm_gain, norm_shift, merge_in_bias, merge_out_bias, query_bias, key_value_bias, rms_gain]
    sizes = [piece.shape[0] for piece in pieces]
    vecs = sum(
        jnp.pad(piece.astype(F32), (sum(sizes[:i]), sum(sizes[i + 1 :])))[None, :]
        for i, piece in enumerate(pieces)
    )
    part, text_rows, text_last = merger(
        image_offsets, vecs, patches, merge_in_weight, merge_out_weight, text_embeds
    )
    queries, shard, embeds = spread(
        image_offsets,
        patch_counts,
        vecs,
        cosine,
        sine,
        part,
        text_rows,
        text_last,
        text_embeds,
        query_weight,
        key_weight,
        value_weight,
    )
    return (embeds, attention(queries, shard))


def solution(mesh):
    placed = (
        P("seq", None),
        P(),
        P(),
        P(None, ("section", "mp")),
        P(("section", "mp")),
        P(("section", "mp"), "seq"),
        P("seq"),
        P("seq", "mp"),
        P(),
        P(None, ("section", "mp")),
        P(("section", "mp")),
        P(None, "mp"),
        P("mp"),
        P(None, "mp"),
        P("mp"),
        P(),
        P(),
    )
    return jax.shard_map(
        local,
        mesh=mesh,
        in_specs=placed,
        out_specs=(P("seq", "mp"), P("seq", ("section", "mp"))),
        check_vma=False,
    )
```

time: 204 us -> 196 us (0.961)
  local copies, waits for them, and re-layouts: 11.1 us -> 4.19 us
  starting transfers between devices: 2.28 us -> 0 us
    pallas_call x2 -> x1, Pallas kernels: 51 us -> 85.4 us  [merger(): pl.pallas_call(merger_kernel, in_specs=[pl.BlockSpec(memory_space=pltpu.S...]
    pallas_call x1, Pallas kernels: 92.8 us -> 66 us  [spread(): pl.pallas_call(spread_kernel, out_shape=[jax.ShapeDtypeStruct((384, 512),...]
    pallas_call x1, Pallas kernels: 41.4 us -> 35.8 us  [attention(): pl.pallas_call(attention_kernel, out_shape=jax.ShapeDtypeStruct(queries.s...]
    broadcast_in_dim x4 -> x0, local copies, waits for them, and re-layouts: 2.5 us -> none  [the longest x1 0.72 us: local(): visual_mask = jnp.broadcast_to(is_visual[:, None].astype(F32), (96, 256))]
    ppermute x1 -> x0, starting transfers between devices: 2.28 us -> none  [local(): lax.ppermute(lax.dynamic_index_in_dim(halves, 1 - section, 1, keepdims=Fa...]
    unnamed x28 -> x4, local copies, waits for them, and re-layouts: 5.16 us -> 3.53 us
  transfers between devices with their start and end apart: 1 -> 0, of which waited for: 0 -> 0; matrix products, arithmetic and copies ran while one was open for 3% -> 0% of each run, Pallas kernels for 6% -> 0%
where the time goes in v3:
time: 196 us; the launch traced here: 195 us
  Pallas kernels  187 us (95%)
  local copies, waits for them, and re-layouts  4.19 us (2%)
  other arithmetic  2.98 us (2%)
    pallas_call x1, Pallas kernels, merger(): pl.pallas_call(merger_kernel, in_specs=[pl.BlockSpec(memory_space=pltpu.S...  85.4 us
    pallas_call x1, Pallas kernels, spread(): pl.pallas_call(spread_kernel, out_shape=[jax.ShapeDtypeStruct((384, 512),...  66 us
    pallas_call x1, Pallas kernels, attention(): pl.pallas_call(attention_kernel, out_shape=jax.ShapeDtypeStruct(queries.s...  35.8 us

profile of v3, /device:TPU:105, one launch (start us, length us, event | category | flops | bytes accessed | tf_op | source)
XLA Modules:
  0.0 195.0 jit_solution(9517605137281692951)
XLA Ops:
  0.6 0.7 broadcast_select_fusion
  1.3 0.8 convert_add_fusion
  2.1 0.7 add.65.vecs
  2.8 1.5 fusion
  4.3 85.4 %merger.1 = (bf16[3,16,4,32,256]{4,3,2,1,0:T(8,128)(2,1)}, bf16[4,64,2048]{2,1,0:T(8,128)(2,1)}, bf16[4,128,2048]{2,1,0:T(8,128)(2,1)}) custom-call(s32[16]{0:T(128)} %offsets.3, f32[1,12544]{1,0:T(1,128)} %add.65.vecs, bf16[1024,1280]{1,0:T(8,128)(2,1)} %patches_ref.1, bf16[5120,640]{1,0:T(8,128)(2,1)} %w_in_ref.1, bf16[640,512]{1,0:T(8,128)(2,1)} %w_out_ref.1, ...), custom_call_target="tpu_custom_call" | custom-call | tf_op jit(solution)/shard_map/merger/pallas_call | solution.py:480
  89.7 66.0 %spread.1 = (bf16[384,512]{1,0:T(8,128)(2,1)}, bf16[384,128]{1,0:T(8,128)(2,1)}, bf16[384,2048]{1,0:T(8,128)(2,1)}) custom-call(s32[16]{0:T(128)} %offsets.3, s32[16]{0:T(128)} %counts.1, f32[1,12544]{1,0:T(1,128)} %add.65.vecs, f32[384,128]{1,0:T(8,128)} %get-tuple-element.15.cos_ref, f32[384,128]{1,0:T(8,128)} %get-tuple-element.14.sin_ref, ...), custom_call_target="tpu_custom_call" | custom-call | tf_op jit(solution)/shard_map/spread/pallas_call | solution.py:721
  155.7 35.8 %attention.1 = bf16[384,512]{1,0:T(8,128)(2,1)} custom-call(bf16[384,512]{1,0:T(8,128)(2,1)} %get-tuple-element.12.q_ref, bf16[384,128]{1,0:T(8,128)(2,1)} %get-tuple-element.13.shard), custom_call_target="tpu_custom_call" | custom-call | tf_op jit(solution)/shard_map/attention/pallas_call | solution.py:817
  191.5 0.0 copy-start
  191.5 2.8 %copy.21 = bf16[384,2048]{1,0:T(8,128)(2,1)} copy(bf16[384,2048]{1,0:T(8,128)(2,1)} %get-tuple-element.20) | data formatting | bytes 3145728
  194.3 0.0 copy-done
  194.3 0.7 copy.22
  (2 shorter events, 0.0 us)
Async XLA Ops:
  191.5 2.8 %copy-start = (bf16[384,512]{1,0:T(8,128)(2,1)S(1)}, bf16[384,512]{1,0:T(8,128)(2,1)}, u32[]{:S(2)}) copy-start(bf16[384,512]{1,0:T(8,128)(2,1)} %attention.1) | copy-start | bytes 1179652

commit v4 on v3

--- a/solution.py
+++ b/solution.py
@@ -427,10 +427,10 @@
         pass
     stage(2)
     stage(3)
+    cross.pass_on(2)
+    cross.pass_on(3)
     unstage(0)
     unstage(1)
-    cross.pass_on(2)
-    cross.pass_on(3)
     cross.add_up(2)
     cross.add_up(3)
     cross.spread(2)
@@ -694,14 +694,14 @@
     place_rows(1)
     start_rows(1)
     relay_rows(0)
+    relay_rows(1)
+    load_q.wait()
+    pltpu.make_async_copy(wk_ref, wkv, load_sem.at[2]).wait()
+    project(0)
     for load in load_last:
         load.wait()
     place_rows(2)
-    relay_rows(1)
-    load_q.wait()
-    pltpu.make_async_copy(wk_ref, wkv, load_sem.at[2]).wait()
     project(2)
-    project(0)
     project(1)
     save = pltpu.make_async_copy(e_out, e_hbm, load_sem.at[4])
     save.start()

time: 196 us -> 196 us (level)
  no operation moved by 1% of the time
where the time goes in v4:
time: 196 us; the launch traced here: 195 us
  Pallas kernels  188 us (96%)
  local copies, waits for them, and re-layouts  4.19 us (2%)
  other arithmetic  2.98 us (2%)
    pallas_call x1, Pallas kernels, merger(): pl.pallas_call(merger_kernel, in_specs=[pl.BlockSpec(memory_space=pltpu.S...  85.4 us
    pallas_call x1, Pallas kernels, spread(): pl.pallas_call(spread_kernel, out_shape=[jax.ShapeDtypeStruct((384, 512),...  64.4 us
    pallas_call x1, Pallas kernels, attention(): pl.pallas_call(attention_kernel, out_shape=jax.ShapeDtypeStruct(queries.s...  37.7 us

profile of v4, /device:TPU:105, one launch (start us, length us, event | category | flops | bytes accessed | tf_op | source)
XLA Modules:
  0.0 195.4 jit_solution(13714145026551498961)
XLA Ops:
  0.6 0.7 broadcast_select_fusion
  1.3 0.8 convert_add_fusion
  2.1 0.7 add.65.vecs
  2.8 1.5 fusion
  4.3 85.4 %merger.1 = (bf16[3,16,4,32,256]{4,3,2,1,0:T(8,128)(2,1)}, bf16[4,64,2048]{2,1,0:T(8,128)(2,1)}, bf16[4,128,2048]{2,1,0:T(8,128)(2,1)}) custom-call(s32[16]{0:T(128)} %offsets.3, f32[1,12544]{1,0:T(1,128)} %add.65.vecs, bf16[1024,1280]{1,0:T(8,128)(2,1)} %patches_ref.1, bf16[5120,640]{1,0:T(8,128)(2,1)} %w_in_ref.1, bf16[640,512]{1,0:T(8,128)(2,1)} %w_out_ref.1, ...), custom_call_target="tpu_custom_call" | custom-call | tf_op jit(solution)/shard_map/merger/pallas_call | solution.py:480
  89.7 64.4 %spread.1 = (bf16[384,512]{1,0:T(8,128)(2,1)}, bf16[384,128]{1,0:T(8,128)(2,1)}, bf16[384,2048]{1,0:T(8,128)(2,1)}) custom-call(s32[16]{0:T(128)} %offsets.3, s32[16]{0:T(128)} %counts.1, f32[1,12544]{1,0:T(1,128)} %add.65.vecs, f32[384,128]{1,0:T(8,128)} %get-tuple-element.15.cos_ref, f32[384,128]{1,0:T(8,128)} %get-tuple-element.14.sin_ref, ...), custom_call_target="tpu_custom_call" | custom-call | tf_op jit(solution)/shard_map/spread/pallas_call | solution.py:721
  154.1 37.7 %attention.1 = bf16[384,512]{1,0:T(8,128)(2,1)} custom-call(bf16[384,512]{1,0:T(8,128)(2,1)} %get-tuple-element.12.q_ref, bf16[384,128]{1,0:T(8,128)(2,1)} %get-tuple-element.13.shard), custom_call_target="tpu_custom_call" | custom-call | tf_op jit(solution)/shard_map/attention/pallas_call | solution.py:817
  191.9 0.0 copy-start
  191.9 2.8 %copy.21 = bf16[384,2048]{1,0:T(8,128)(2,1)} copy(bf16[384,2048]{1,0:T(8,128)(2,1)} %get-tuple-element.20) | data formatting | bytes 3145728
  194.7 0.0 copy-done
  194.7 0.7 copy.22
  (2 shorter events, 0.0 us)
Async XLA Ops:
  191.9 2.8 %copy-start = (bf16[384,512]{1,0:T(8,128)(2,1)S(1)}, bf16[384,512]{1,0:T(8,128)(2,1)}, u32[]{:S(2)}) copy-start(bf16[384,512]{1,0:T(8,128)(2,1)} %attention.1) | copy-start | bytes 1179652
